TPU v7x, 256 devices: a whole 4x4x8 slice. The times are simulated.
256 devices in a mesh: row: 16 (over z_hi, x, core), col: 16 (over z_lo, y).
Axes of the slice: x: 4, y: 4, z: 8 (z_hi: 2, z_lo: 4; z = z_hi * 4 + z_lo), core: 2. Of those that a mesh axis runs over, the one named last changes fastest.
Arguments:
- matrix: float32 [16384, 16384], P('row', 'col'), as said below
Outputs:
- updated: float32 [16384, 16384], P('row', 'col')
- r_factor: float32 [256, 256], replicated
Inputs may be any that keep to these rules, and one draw needn't show every extreme that they name: matrix is symmetric once read in global order; its entries are of order one, those of a symmetric normal matrix, possibly plus a small symmetric rank-one term, scaled on both sides by row factors between 0.3 and 3.
All inputs are finite; a program needn't handle non-finite values.
Results may differ from a plain program's by a relative error of at most 0.00013.
Values sent between devices are 32-bit elements; how exact they have to be, the bound alone decides.
A program may use at most 128 MiB of HBM per device.

v0:
```python
import jax
import jax.numpy as jnp
from jax import lax
from jax.sharding import PartitionSpec as P

NB = 256


def broadcast(array, axis, root):
    mine = lax.axis_index(axis) == root
    return lax.psum(jnp.where(mine, array, jnp.zeros_like(array)), axis)


def product(left, right):
    return jnp.dot(left, right, precision=lax.Precision.HIGHEST, preferred_element_type=jnp.float32)


def contract_first(left, right):
    return lax.dot_general(
        left,
        right,
        (((0,), (0,)), ((), ())),
        precision=lax.Precision.HIGHEST,
        preferred_element_type=jnp.float32,
    )


def contract_last(left, right):
    return lax.dot_general(
        left,
        right,
        (((1,), (1,)), ((), ())),
        precision=lax.Precision.HIGHEST,
        preferred_element_type=jnp.float32,
    )


def pick_gathered(whole, row_count, col_index, col_blocks):
    breadth = whole.shape[1]
    per_row = whole.shape[0] // row_count // NB
    grouped = whole.reshape(row_count, per_row, NB, breadth).transpose(1, 0, 2, 3)
    chosen = lax.dynamic_index_in_dim(grouped, col_index, 1, keepdims=False)
    return chosen.reshape(col_blocks * NB, breadth)


def on_device(matrix):
    row_count = lax.axis_size("row")
    row_index = lax.axis_index("row")
    col_index = lax.axis_index("col")
    local_rows = matrix.shape[0]
    col_blocks = matrix.shape[1] // NB
    panel = broadcast(matrix[:, :NB], "col", 0)
    block_ids = jnp.arange(local_rows, dtype=jnp.int32) // NB * row_count + row_index
    panel = jnp.where((block_ids > 0)[:, None], panel, jnp.float32(0.0))
    gram = lax.psum(contract_first(panel, panel), "row")
    lower = jnp.linalg.cholesky(gram)
    q_rows = lax.linalg.triangular_solve(
        lower, panel, left_side=False, lower=True, transpose_a=True
    )
    whole = lax.all_gather(q_rows, "row", axis=0, tiled=True)
    q_cols = pick_gathered(whole, row_count, col_index, col_blocks)
    image_part = product(matrix, q_cols)
    image_rows = lax.psum(image_part, "col")
    curvature = lax.psum(contract_first(q_rows, image_rows), "row")
    sweep_rows = 2.0 * image_rows - 2.0 * product(q_rows, curvature)
    image_cols = lax.psum(contract_first(q_rows, matrix), "row")
    sweep_cols = 2.0 * image_cols - 2.0 * contract_last(curvature.T, q_cols)
    updated = matrix - product(q_rows, sweep_cols) - contract_last(sweep_rows, q_cols)
    return (updated, lower.T)


def solution(mesh):
    return jax.shard_map(
        on_device,
        mesh=mesh,
        in_specs=(P("row", "col"),),
        out_specs=(P("row", "col"), P()),
        check_vma=False,
    )
```

profile of v0, /device:TPU:1, one launch (start us, length us, event | category | flops | bytes accessed | tf_op | source)
XLA Modules:
  0.0 984.7 jit_solution(9015573758776528663)
XLA Ops:
  7.2 0.0 all-reduce.7.cloned.1.call-start
  7.2 2.3 slice_select_fusion
  9.5 0.0 all-reduce.7.cloned.1.call-update
  9.5 0.0 all-reduce.9.cloned.1.call-start
  9.6 158.3 %all-reduce.7.cloned.1.call-done = f32[1024,256]{1,0:T(8,128)} async-done(((f32[1024,256]{1,0:T(8,128)}), f32[1024,256]{1,0:T(8,128)}) %all-reduce.7.cloned.1.call-update) | async-done | bytes 1048592 | tf_op jit(solution)/shard_map/psum | solution.py:11
  167.9 1.4 broadcast_select_fusion
  169.3 2.5 fusion.22
  171.8 0.0 all-reduce.9.cloned.1.call-update
  171.8 0.2 all-gather.2.cloned.1.call-start
  172.1 184.7 %all-reduce.9.cloned.1.call-done = f32[256,256]{0,1:T(8,128)} async-done(((f32[256,256]{0,1:T(8,128)}), f32[256,256]{0,1:T(8,128)}) %all-reduce.9.cloned.1.call-update) | async-done | bytes 262160 | tf_op jit(solution)/shard_map/psum | solution.py:55
  356.8 1.1 copy.4
  357.9 1.0 fusion.4
  358.9 11.7 %cholesky.50 = f32[128,128]{1,0:T(8,128)S(1)} custom-call(f32[128,128]{1,0:T(8,128)S(1)} %cholesky.118), custom_call_target="Cholesky" | custom-call | tf_op jit(solution)/shard_map/jit(cholesky)/cholesky | solution.py:56
  370.7 9.8 custom-call.14
  380.5 0.2 constant_dynamic-update-slice_fusion.1
  380.7 0.3 convolution_subtract_fusion.1
  381.0 11.7 %cholesky.105 = f32[128,128]{1,0:T(8,128)S(1)} custom-call(f32[128,128]{1,0:T(8,128)S(1)} %convolution_subtract_fusion.1), custom_call_target="Cholesky" | custom-call | tf_op jit(solution)/shard_map/jit(cholesky)/cholesky | solution.py:56
  392.8 0.7 compare_reduce_fusion
  394.7 0.1 triangular_solve.58
  394.8 4.1 while.1
  395.0 0.6 fusion.40
  395.6 1.4 bitcast_dynamic-update-slice_fusion.2
  397.0 0.6 fusion.40
  397.5 1.4 bitcast_dynamic-update-slice_fusion.2
  398.9 19.7 %custom-call.15 = f32[2,128,128]{1,2,0:T(8,128)S(1)} custom-call(f32[2,128,128]{2,1,0:T(8,128)S(1)} %get-tuple-element.9), custom_call_target="InvertDiagBlocksLowerTriangular" | custom-call | tf_op jit(solution)/shard_map/triangular_solve | solution.py:57
  418.6 0.6 fusion.2
  419.2 1.0 convolution_subtract_fusion
  420.2 0.6 fusion.7
  420.8 1.0 pad_maximum_fusion
  421.9 0.0 all-gather.2.cloned.1.call-update
  421.9 0.0 all-reduce.11.cloned.1.call-start
  422.0 176.0 %all-gather.2.cloned.1.call-done = f32[16384,256]{0,1:T(8,128)} async-done(((f32[1024,256]{0,1:T(8,128)}), f32[16384,256]{0,1:T(8,128)}) %all-gather.2.cloned.1.call-update) | async-done | bytes 16777232 | tf_op jit(solution)/shard_map/all_gather | solution.py:60
  598.0 20.4 %reshape.46 = f32[16,4,256,256]{2,1,0,3:T(4,128)} reshape(f32[16384,256]{0,1:T(8,128)} %all-gather.2.cloned.1.call-done) | data formatting | bytes 33554432 | tf_op jit(solution)/shard_map/reshape | solution.py:41
  618.4 0.0 copy-start
  618.4 1.6 constant_dynamic-slice_fusion.1
  620.0 0.2 copy.7
  620.2 0.8 copy-done
  620.9 4.7 convolution_bitcast_fusion
  625.6 0.0 all-reduce.11.cloned.1.call-update
  625.7 0.3 all-reduce.13.cloned.1.call-start
  626.0 6.9 fusion.20
  632.8 140.0 %all-reduce.11.cloned.1.call-done = f32[1024,256]{0,1:T(8,128)} async-done(((f32[1024,256]{0,1:T(8,128)}), f32[1024,256]{0,1:T(8,128)}) %all-reduce.11.cloned.1.call-update) | async-done | bytes 1048592 | tf_op jit(solution)/shard_map/psum | solution.py:63
  772.9 3.0 fusion.19
  775.8 0.0 all-reduce.13.cloned.1.call-update
  775.9 0.8 copy.5
  776.7 189.0 %all-reduce.13.cloned.1.call-done = (f32[256,256]{1,0:T(8,128)}, f32[256,1024]{1,0:T(8,128)}) async-done(((f32[256,256]{1,0:T(8,128)}, f32[256,1024]{1,0:T(8,128)}), (f32[256,256]{1,0:T(8,128)}, f32[256,1024]{1,0:T(8,128)})) %all-reduce.13.cloned.1.call-update) | async-done | bytes 1310736 | tf_op jit(solution)/shard_map/psum | solution.py:64
  965.7 0.0 copy-start.2
  965.7 0.0 copy-start.3
  965.7 2.5 fusion.1
  968.2 0.0 copy-start.1
  968.2 3.5 fusion.18
  971.8 0.0 copy-done.2
  971.8 0.0 copy-done.3
  971.8 1.2 fusion
  973.0 0.0 copy-done.1
  973.0 5.2 subtract_subtract_fusion
  (10 shorter events, 0.2 us)
Async XLA Ops:
  7.2 160.7 %all-reduce.7.cloned.1.call-start = ((), (), s32[]{:S(2)}) async-start(), calls=%async_computation | async-start | bytes 2097152 | tf_op jit(solution)/shard_map/psum | solution.py:11
  9.5 347.3 %all-reduce.9.cloned.1.call-start = ((), (), s32[]{:S(2)}) async-start(), calls=%async_computation.1 | async-start | bytes 524288 | tf_op jit(solution)/shard_map/psum | solution.py:55
  171.8 426.1 %all-gather.2.cloned.1.call-start = ((), (), s32[]{:S(2)}) async-start(), calls=%async_computation.2 | async-start | bytes 17825792 | tf_op jit(solution)/shard_map/all_gather | solution.py:60
  421.9 351.0 %all-reduce.11.cloned.1.call-start = ((), (), s32[]{:S(2)}) async-start(), calls=%async_computation.3 | async-start | bytes 2097152 | tf_op jit(solution)/shard_map/psum | solution.py:63
  618.4 2.5 copy-start
  625.7 340.0 %all-reduce.13.cloned.1.call-start = ((), (), s32[]{:S(2)}) async-start(), calls=%async_computation.4 | async-start | bytes 2621440 | tf_op jit(solution)/shard_map/psum | solution.py:64
  965.7 6.1 copy-start.2
  965.7 6.1 copy-start.3
  968.2 4.8 copy-start.1
Sparse Core Ops, SparseCore 0:
  11.2 156.6 all-reduce.6
  172.0 184.8 all-reduce.8
  422.0 175.9 all-gather.1
  625.8 147.0 all-reduce.10
  776.2 189.4 all-reduce.12
where the time goes:
time: 986 us; the launch traced here: 985 us
  waiting for transfers between devices  848 us (86%)
  other arithmetic  59.4 us (6%)
  matrix products  32.2 us (3%)
  local copies, waits for them, and re-layouts  28.9 us (3%)
  between operations  15.2 us (2%)
    psum x1, waiting for transfers between devices, on_device(): curvature = lax.psum(contract_first(q_rows, image_rows), 'row')  189 us
    psum x1, waiting for transfers between devices, on_device(): gram = lax.psum(contract_first(panel, panel), 'row')  185 us
    all_gather x1, waiting for transfers between devices, on_device(): whole = lax.all_gather(q_rows, 'row', axis=0, tiled=True)  176 us
    psum x1, waiting for transfers between devices, broadcast(): return lax.psum(jnp.where(mine, array, jnp.zeros_like(array)), axis)  158 us
    psum x1, waiting for transfers between devices, on_device(): image_rows = lax.psum(image_part, 'col')  140 us
    another operation x6, other arithmetic, on_device(): lower = jnp.linalg.cholesky(gram)  34 us
    another operation x3, other arithmetic, on_device(): lax.linalg.triangular_solve(lower, panel, left_side=False, lower=True, tr...  20.7 us
    reshape x1, local copies, waits for them, and re-layouts, pick_gathered(): whole.reshape(row_count, per_row, NB, breadth).transpose(1, 0, 2, 3)  20.4 us
  transfers between devices with their start and end apart: 5, of which 5 were waited for; matrix products, arithmetic and copies ran while one was open for 1% of the time, Pallas kernels for 0%

commit v1 on v0

v1 whole, which is shorter than its diff:
```python
import functools
import jax
import jax.numpy as jnp
from jax import lax
from jax.experimental import pallas as pl
from jax.experimental.pallas import tpu as pltpu
from jax.sharding import PartitionSpec as P

NB = 256
N = 1024
CH = 16
MESH = pl.DeviceIdType.MESH
F32 = jnp.float32
BF16 = jnp.bfloat16

LAST = (((1,), (1,)), ((), ()))
FIRST = (((0,), (0,)), ((), ()))
PLAIN = (((1,), (0,)), ((), ()))


def split(x):
    hi = x.astype(BF16)
    lo = (x - hi.astype(F32)).astype(BF16)
    return hi, lo


def dot(a, b, dims):
    return lax.dot_general(a, b, dims, preferred_element_type=F32)


def dot3s(a, b, dims):
    (ah, al), (bh, bl) = a, b
    return dot(ah, bh, dims) + (dot(ah, bl, dims) + dot(al, bh, dims))


def dot3(a, b, dims):
    return dot3s(split(a), split(b), dims)


def dot6(a, b, dims):
    return lax.dot_general(a, b, dims, precision=lax.Precision.HIGHEST, preferred_element_type=F32)


def chunk(k):
    return pl.ds(pl.multiple_of(k * CH, CH), CH)


class Sends:
    def __init__(self, sems):
        self.sems = sems
        self.count = 0
        self.pending = []

    def go(self, src, dst, recv, dev, cond=None):
        copy = pltpu.make_async_remote_copy(
            src_ref=src, dst_ref=dst, send_sem=self.sems.at[self.count], recv_sem=recv, device_id=dev, device_id_type=MESH
        )
        self.count += 1
        self.pending.append((copy, cond))
        when(cond, copy.start)

    def drain(self):
        for copy, cond in self.pending:
            when(cond, copy.wait_send)
        self.pending = []


def when(cond, fn):
    if cond is None:
        fn()
    else:
        pl.when(cond)(fn)


def arrived(ref, recv, send, cond=None):
    copy = pltpu.make_async_copy(ref, ref, recv)
    when(cond, copy.wait)


def exchange_kernel(
    s_hbm, pr, pc, wr, wc, gf, cf,
    s, wp, r1, t, r2, u, r3, gp, grs, crs,
    load_sem, send_sem, gsend, gasend, csend, casend,
    pr_sem, pc_sem, wr_sem, wc_sem, r1_sem, r2_sem, r3_sem, grs_sem, gf_sem, crs_sem, cf_sem,
):
    p = lax.axis_index("row")
    q = lax.axis_index("col")
    zh, x, c = p // 8, (p // 2) % 4, p % 2
    zl, y = q // 4, q % 4

    load = pltpu.make_async_copy(s_hbm, s, load_sem)
    load.start()

    def row_of(zh_, x_, c_):
        return zh_ * 8 + x_ * 2 + c_

    barrier = pltpu.get_barrier_semaphore()

    def greet(i, carry):
        pl.semaphore_signal(barrier, inc=1, device_id=(lax.rem(p + i, 16), q), device_id_type=MESH)
        pl.semaphore_signal(barrier, inc=1, device_id=(p, lax.rem(q + i, 16)), device_id_type=MESH)
        return carry

    lax.fori_loop(1, 16, greet, 0)

    @pl.when(p != q)
    def _():
        pl.semaphore_signal(barrier, inc=1, device_id=(q, p), device_id_type=MESH)
        pl.semaphore_wait(barrier, 31)

    @pl.when(p == q)
    def _():
        pl.semaphore_wait(barrier, 30)

    load.wait()
    out = Sends(send_sem)


    def col_start(buf, sems, root):
        for i in (1, 2, 3):
            d = lax.rem(zl + i, 4) * 4 + y
            out.go(buf.at[chunk(q)], buf.at[chunk(q)], sems.at[q], (p, d), (d != 0) if root else None)
        for i in (1, 3, 2):
            d = zl * 4 + lax.rem(y + i, 4)
            out.go(buf.at[chunk(q)], buf.at[chunk(q)], sems.at[q], (p, d), (d != 0) if root else None)

    def col_forward(buf, sems, root):
        for i in (1, 3, 2):
            k = lax.rem(zl + i, 4) * 4 + y
            arrived(buf.at[chunk(k)], sems.at[k], None, (q != 0) if root else None)
            for j in (1, 3, 2):
                d = zl * 4 + lax.rem(y + j, 4)
                out.go(buf.at[chunk(k)], buf.at[chunk(k)], sems.at[k], (p, d), (d != 0) if root else None)

    def col_finish(buf, sems, root):
        for i in (0, 1, 3, 2):
            for j in (1, 3, 2):
                k = lax.rem(zl + i, 4) * 4 + lax.rem(y + j, 4)
                arrived(buf.at[chunk(k)], sems.at[k], None, (q != 0) if root else None)

    def row_send(buf, sems, k, d, root):
        out.go(buf.at[chunk(k)], buf.at[chunk(k)], sems.at[k], (d, q), (d != 0) if root else None)

    def row_start(buf, sems, root):
        row_send(buf, sems, p, row_of(1 - zh, x, c), root)
        for i in (1, 3, 2):
            row_send(buf, sems, p, row_of(zh, lax.rem(x + i, 4), c), root)
        row_send(buf, sems, p, row_of(zh, x, 1 - c), root)

    def row_partner(buf, sems, root):
        k = row_of(1 - zh, x, c)
        arrived(buf.at[chunk(k)], sems.at[k], None, (p != 0) if root else None)
        for i in (1, 3, 2):
            row_send(buf, sems, k, row_of(zh, lax.rem(x + i, 4), c), root)
        row_send(buf, sems, k, row_of(zh, x, 1 - c), root)

    def row_own(buf, sems, root, z):
        for i in (1, 3, 2):
            k = row_of(z, lax.rem(x + i, 4), c)
            arrived(buf.at[chunk(k)], sems.at[k], None, (p != 0) if root else None)
            row_send(buf, sems, k, row_of(zh, x, 1 - c), root)

    def row_finish(buf, sems, root):
        for z in (zh, 1 - zh):
            for i in (0, 1, 3, 2):
                k = row_of(z, lax.rem(x + i, 4), 1 - c)
                arrived(buf.at[chunk(k)], sems.at[k], None, (p != 0) if root else None)

    lane = lax.broadcasted_iota(jnp.int32, (NB, N), 1)

    @pl.when(p == 0)
    def _():
        pc[...] = jnp.where((q == 0) & (lane < NB), 0.0, s[0:NB, :])

    for k in (14, 15, 12, 13, 10, 11, 8, 9, 6, 7, 4, 5, 2, 3, 1):
        out.go(pc.at[chunk(k)], pc.at[chunk(k)], pc_sem.at[k], (k, q), p == 0)

    @pl.when(q == 0)
    def _():
        pr[...] = jnp.where((p == 0) & (lane < NB), 0.0, s[:, 0:NB].T)

    for k in (15, 14, 13, 12, 11, 10, 9, 8, 7, 6, 5, 4, 3, 2, 1):
        out.go(pr.at[chunk(k)], pr.at[chunk(k)], pr_sem.at[k], (p, k), q == 0)

    arrived(pr.at[chunk(q)], pr_sem.at[q], None, q != 0)
    col_start(pr, pr_sem, True)
    arrived(pc.at[chunk(p)], pc_sem.at[p], None, p != 0)
    row_start(pc, pc_sem, True)
    col_forward(pr, pr_sem, True)
    row_partner(pc, pc_sem, True)
    row_own(pc, pc_sem, True, zh)
    row_own(pc, pc_sem, True, 1 - zh)
    row_finish(pc, pc_sem, True)

    gp[...] = dot3(pc[...], pc[...], LAST)
    grs[pl.ds(q, 1)] = gp[chunk(q), :][None]

    def direct(i, src, dst, ssem, rsem, dev):
        return pltpu.make_async_remote_copy(
            src_ref=src, dst_ref=dst, send_sem=ssem, recv_sem=rsem, device_id=dev, device_id_type=MESH
        )

    def gram_copy(i):
        d = lax.rem(q + i, 16)
        return direct(i, gp.at[chunk(d)], grs.at[q], gsend.at[i], grs_sem.at[q], (p, d))

    def gram_all(i):
        d = lax.rem(q + i, 16)
        return direct(i, gf.at[chunk(q)], gf.at[chunk(q)], gasend.at[i], gf_sem.at[q], (p, d))

    def curv_copy(i):
        d = lax.rem(q + i, 16)
        return direct(i, crs.at[q], crs.at[q], csend.at[i], crs_sem.at[q], (p, d))

    def curv_all(i):
        d = lax.rem(p + i, 16)
        return direct(i, cf.at[chunk(p)], cf.at[chunk(p)], casend.at[i], cf_sem.at[p], (d, q))

    def start_all(make):
        lax.fori_loop(1, 16, lambda i, z: (make(i).start(), z)[1], 0)

    def drain_all(make):
        lax.fori_loop(1, 16, lambda i, z: (make(i).wait_send(), z)[1], 0)

    def wait_slots(buf, sems, me):
        def step(i, z):
            k = lax.rem(me + i, 16)
            arrived(buf.at[k], sems.at[k], None)
            return z

        lax.fori_loop(1, 16, step, 0)

    def wait_chunks(buf, sems, me):
        def step(i, z):
            k = lax.rem(me + i, 16)
            arrived(buf.at[chunk(k)], sems.at[k], None)
            return z

        lax.fori_loop(1, 16, step, 0)

    start_all(gram_copy)
    col_finish(pr, pr_sem, True)

    ph, plo = split(pr[...])
    wp4 = wp.reshape(NB, N)

    def product(j, z):
        cols = pl.ds(pl.multiple_of(j * 256, 256), 256)
        wp4[:, cols] = dot3s((ph, plo), split(s[:, cols]), PLAIN)
        return z

    lax.fori_loop(0, 4, product, 0)

    out.go(wp.at[:, 1 - c], r1, r1_sem, (row_of(zh, x, 1 - c), q))

    wait_slots(grs, grs_sem, q)
    gf[chunk(q), :] = jnp.sum(grs[...], axis=0)
    start_all(gram_all)

    arrived(r1, r1_sem, None)
    t[...] = wp[:, pl.ds(c, 1)][:, 0] + r1[...]
    for phase, z in ((0, 1 - zh), (1, zh)):
        for i in (1, 3, 2):
            xx = lax.rem(x + i, 4)
            out.go(t.at[z * 4 + xx], r2.at[phase, i - 1], r2_sem.at[phase, i - 1], (row_of(zh, xx, c), q))
    for i in (1, 3, 2):
        arrived(r2.at[0, i - 1], r2_sem.at[0, i - 1], None)
    u[...] = t[(1 - zh) * 4 + x] + (r2[0, 0] + r2[0, 1] + r2[0, 2])
    out.go(u, r3, r3_sem, (row_of(1 - zh, x, c), q))
    for i in (1, 3, 2):
        arrived(r2.at[1, i - 1], r2_sem.at[1, i - 1], None)
    part = t[zh * 4 + x] + (r2[1, 0] + r2[1, 1] + r2[1, 2])
    arrived(r3, r3_sem, None)
    mine = part + r3[...]
    wc[chunk(p), :] = mine

    out.go(wc.at[chunk(p)], wr.at[chunk(p)], wr_sem.at[p], (q, p), p != q)

    @pl.when(p == q)
    def _():
        wr[chunk(q), :] = mine

    row_start(wc, wc_sem, False)
    crs[pl.ds(q, 1)] = dot3(mine, pc[...], LAST)[None]
    start_all(curv_copy)
    arrived(wr.at[chunk(q)], wr_sem.at[q], None, p != q)
    col_start(wr, wr_sem, False)
    row_partner(wc, wc_sem, False)
    row_own(wc, wc_sem, False, zh)
    col_forward(wr, wr_sem, False)
    wait_slots(crs, crs_sem, q)
    cf[chunk(p), :] = jnp.sum(crs[...], axis=0)
    start_all(curv_all)
    row_own(wc, wc_sem, False, 1 - zh)
    row_finish(wc, wc_sem, False)
    wait_chunks(gf, gf_sem, q)
    wait_chunks(cf, cf_sem, p)
    col_finish(wr, wr_sem, False)
    out.drain()
    for make in (gram_copy, gram_all, curv_copy, curv_all):
        drain_all(make)


def exchange(matrix):
    vm = pl.BlockSpec(memory_space=pltpu.VMEM)
    dma = pltpu.SemaphoreType.DMA
    big = jax.ShapeDtypeStruct((NB, N), F32)
    small = jax.ShapeDtypeStruct((NB, NB), F32)
    return pl.pallas_call(
        exchange_kernel,
        out_shape=(big, big, big, big, small, small),
        in_specs=[pl.BlockSpec(memory_space=pl.ANY)],
        out_specs=(vm,) * 6,
        scratch_shapes=[
            pltpu.VMEM((N, N), F32),
            pltpu.VMEM((8, 2, CH, N), F32),
            pltpu.VMEM((8, CH, N), F32),
            pltpu.VMEM((8, CH, N), F32),
            pltpu.VMEM((2, 3, CH, N), F32),
            pltpu.VMEM((CH, N), F32),
            pltpu.VMEM((CH, N), F32),
            pltpu.VMEM((NB, NB), F32),
            pltpu.VMEM((16, CH, NB), F32),
            pltpu.VMEM((16, CH, NB), F32),
            dma, dma((128,)), dma((16,)), dma((16,)), dma((16,)), dma((16,)),
            dma((16,)), dma((16,)), dma((16,)), dma((16,)), dma, dma((2, 3)), dma, dma((16,)), dma((16,)), dma((16,)), dma((16,)),
        ],
        compiler_params=pltpu.CompilerParams(collective_id=0, has_side_effects=True, vmem_limit_bytes=40 << 20),
        name="exchange",
    )(matrix)


def factor(aug):
    b = 64
    row = lax.broadcasted_iota(jnp.int32, (b, 2 * b), 0)
    col = lax.broadcasted_iota(jnp.int32, (b, 2 * b), 1)
    eye = (row + b == col).astype(F32)
    for k in range(4):
        here = slice(k * b, (k + 1) * b)
        a = jnp.concatenate([aug[here, here], eye[:, b:]], axis=1)
        for j in range(0, b, 2):
            c0, c1 = a[:, j : j + 1], a[:, j + 1 : j + 2]
            r0, r1 = a[j : j + 1, :], a[j + 1 : j + 2, :]
            a00, a01, a11 = a[j : j + 1, j : j + 1], a[j : j + 1, j + 1 : j + 2], a[j + 1 : j + 2, j + 1 : j + 2]
            inv = 1.0 / (a00 * a11 - a01 * a01)
            w0 = (a11 * r0 - a01 * r1) * inv
            w1 = (a00 * r1 - a01 * r0) * inv
            rest = c0 * w0 + c1 * w1
            second = (a01 / a00) * r0
            a = a - jnp.where(row > j + 1, rest, jnp.where(row == j + 1, second, 0.0))
        diag = jnp.sum(jnp.where(row == col, a, 0.0), axis=1, keepdims=True)
        inverse = (a * lax.rsqrt(diag))[:, b:]
        done = dot6(inverse, aug[here, :], PLAIN)
        aug[here, :] = done
        if k < 3:
            below = slice((k + 1) * b, NB)
            aug[below, :] = aug[below, :] - dot6(done[:, 0:NB], done, FIRST)[below, :]


def finish_kernel(pr, pc, wr, wc, gf, cf, s, out, r, aug, left, right):
    @pl.when(pl.program_id(0) == 0)
    def _():
        row = lax.broadcasted_iota(jnp.int32, (NB, NB), 0)
        col = lax.broadcasted_iota(jnp.int32, (NB, NB), 1)
        aug[:, 0:NB] = gf[...]
        aug[:, NB:] = (row == col).astype(F32)
        factor(aug)
        r[...] = jnp.where(row <= col, aug[:, 0:NB], 0.0)
        inverse = aug[:, NB:]
        m = split(2.0 * dot6(inverse, inverse, FIRST))
        half = split(0.5 * cf[...])
        for panel, image, side in ((pr, wr, 0), (pc, wc, 1)):
            a = dot3s(m, split(panel[...]), PLAIN)
            v = image[...] - dot3s(half, split(a), PLAIN)
            if side == 0:
                ah, al = split(a.T)
                vh, vl = split(v.T)
                for i, block in enumerate((ah, vh, ah, vh, al, vl)):
                    left[:, i * NB : (i + 1) * NB] = block
            else:
                ah, al = split(a)
                vh, vl = split(v)
                for i, block in enumerate((vh, ah, vl, al, vh, ah)):
                    right[i * NB : (i + 1) * NB, :] = block

    rows = pl.ds(pl.multiple_of(pl.program_id(0) * TILE, TILE), TILE)
    out[...] = s[...] - dot(left[rows, :], right[...], PLAIN)


TILE = 128


def finish(parts, matrix):
    whole = lambda shape: pl.BlockSpec(shape, lambda i: (0, 0))
    big, small, tile = whole((NB, N)), whole((NB, NB)), pl.BlockSpec((TILE, N), lambda i: (i, 0))
    return pl.pallas_call(
        finish_kernel,
        grid=(N // TILE,),
        out_shape=(jax.ShapeDtypeStruct((N, N), F32), jax.ShapeDtypeStruct((NB, NB), F32)),
        in_specs=[big, big, big, big, small, small, tile],
        out_specs=(tile, small),
        scratch_shapes=[pltpu.VMEM((NB, 2 * NB), F32), pltpu.VMEM((N, 6 * NB), BF16), pltpu.VMEM((6 * NB, N), BF16)],
        compiler_params=pltpu.CompilerParams(vmem_limit_bytes=48 << 20),
        name="finish",
    )(*parts, matrix)


def on_device(matrix):
    return finish(exchange(matrix), matrix)


def solution(mesh):
    return jax.shard_map(
        on_device,
        mesh=mesh,
        in_specs=(P("row", "col"),),
        out_specs=(P("row", "col"), P()),
        check_vma=False,
    )
```

time: 986 us -> 137 us (0.14)
  the two profiles are of different devices: /device:TPU:1 before, /device:TPU:32 now
where the time goes in v1:
time: 137 us
  Pallas kernels  134 us (98%)
  local copies, waits for them, and re-layouts  2.18 us (2%)
    pallas_call x1, Pallas kernels, exchange(): pl.pallas_call(exchange_kernel, out_shape=(big, big, big, big, small, sma...  99.2 us
    pallas_call x1, Pallas kernels, finish(): pl.pallas_call(finish_kernel, grid=(N // TILE,), out_shape=(jax.ShapeDtyp...  35 us

profile of v1, /device:TPU:32, one launch (start us, length us, event | category | flops | bytes accessed | tf_op | source)
XLA Modules:
  0.0 137.0 jit_solution(2225308555138885068)
XLA Ops:
  0.6 0.0 copy-start
  0.6 2.2 %copy-done = f32[1024,1024]{1,0:T(8,128)S(1)} copy-done((f32[1024,1024]{1,0:T(8,128)S(1)}, f32[1024,1024]{1,0:T(8,128)}, u32[]{:S(2)}) %copy-start) | copy-done | bytes 4194328
  2.8 99.2 %exchange.1 = (f32[256,1024]{1,0:T(8,128)S(1)}, f32[256,1024]{1,0:T(8,128)S(1)}, f32[256,1024]{1,0:T(8,128)S(1)}, f32[256,1024]{1,0:T(8,128)S(1)}, f32[256,256]{1,0:T(8,128)S(1)}, /*index=5*/f32[256,256]{1,0:T(8,128)S(1)}) custom-call(f32[1024,1024]{1,0:T(8,128)S(1)} %copy-done), custom_call_target="tpu_custom_call" | custom-call | tf_op jit(solution)/shard_map/exchange/pallas_call | solution.py:309
  102.0 35.0 %finish.1 = (f32[1024,1024]{1,0:T(8,128)}, f32[256,256]{1,0:T(8,128)}) custom-call(f32[256,1024]{1,0:T(8,128)S(1)} %get-tuple-element.8.pr, f32[256,1024]{1,0:T(8,128)S(1)} %get-tuple-element.9.pc, f32[256,1024]{1,0:T(8,128)S(1)} %get-tuple-element.10.wr, f32[256,1024]{1,0:T(8,128)S(1)} %get-tuple-element.11.wc, f32[256,256]{1,0:T(8,128)S(1)} %get-tuple-element.12.gf, ...), custom_call_target="tpu_custom_call" | custom-call | tf_op jit(solution)/shard_map/finish/pallas_call | solution.py:396
Async XLA Ops:
  0.6 2.2 %copy-start = (f32[1024,1024]{1,0:T(8,128)S(1)}, f32[1024,1024]{1,0:T(8,128)}, u32[]{:S(2)}) copy-start(f32[1024,1024]{1,0:T(8,128)} %s.1) | copy-start | bytes 12582916

commit v2 on v1

--- a/solution.py
+++ b/solution.py
@@ -77,9 +77,61 @@
     when(cond, copy.wait)
 
 
+def reciprocal(x):
+    y = pl.reciprocal(x, approx=True)
+    return y * (2.0 - x * y)
+
+
+def pivot8(step, a):
+    tiles = [a[8 * t : 8 * t + 8, :] for t in range(8)]
+    sub = lax.broadcasted_iota(jnp.int32, (8, 128), 0)
+    full = lambda v: jnp.broadcast_to(v, (8, 128))
+    cols = [[full(tile[:, i : i + 1]) for i in range(8)] for tile in tiles]
+    e = [[full(cols[0][k][i : i + 1, :]) if k >= i else None for k in range(8)] for i in range(8)]
+    rows = [full(tiles[0][i : i + 1, :]) for i in range(8)]
+    scaled = []
+    for i in range(8):
+        inv = reciprocal(e[i][i])
+        scaled.append(rows[i] * inv)
+        for k in range(i + 1, 8):
+            f = e[i][k] * inv
+            rows[k] = rows[k] - f * rows[i]
+            for n in range(k, 8):
+                e[k][n] = e[k][n] - f * e[i][n]
+            for t in range(1, 8):
+                cols[t][k] = cols[t][k] - cols[t][i] * f
+    top = rows[0]
+    for i in range(1, 8):
+        top = jnp.where(sub == i, rows[i], top)
+    new = []
+    for t in range(1, 8):
+        term = cols[t][0] * scaled[0]
+        for i in range(1, 8):
+            term = term + cols[t][i] * scaled[i]
+        new.append(tiles[t] - term * jnp.where(step + t < 8, 1.0, 0.0).astype(F32))
+    return pltpu.roll(jnp.concatenate(new + [top], axis=0), 120, axis=1)
+
+
+def factor_block(aug, k):
+    b = 64
+    row = lax.broadcasted_iota(jnp.int32, (b, 2 * b), 0)
+    col = lax.broadcasted_iota(jnp.int32, (b, 2 * b), 1)
+    here = slice(k * b, (k + 1) * b)
+    eye = (row + b == col).astype(F32)
+    a = jnp.concatenate([aug[here, here], eye[:, b:]], axis=1)
+    a = lax.fori_loop(0, 8, pivot8, a)
+    diag = jnp.sum(jnp.where(row + b == col, a, 0.0), axis=1, keepdims=True)
+    inverse = (a * lax.rsqrt(diag))[:, :b]
+    done = dot6(inverse, aug[here, :], PLAIN)
+    aug[here, :] = done
+    if k < 3:
+        below = slice((k + 1) * b, NB)
+        aug[below, :] = aug[below, :] - dot6(done[:, (k + 1) * b : NB], done, FIRST)
+
+
 def exchange_kernel(
-    s_hbm, pr, pc, wr, wc, gf, cf,
-    s, wp, r1, t, r2, u, r3, gp, grs, crs,
+    s_hbm, left, right, rfac,
+    pr, pc, wr, wc, gf, cf, s, wp, r1, t, r2, u, r3, gp, grs, crs, aug, ar, ac,
     load_sem, send_sem, gsend, gasend, csend, casend,
     pr_sem, pc_sem, wr_sem, wc_sem, r1_sem, r2_sem, r3_sem, grs_sem, gf_sem, crs_sem, cf_sem,
 ):
@@ -103,15 +155,7 @@
 
     lax.fori_loop(1, 16, greet, 0)
 
-    @pl.when(p != q)
-    def _():
-        pl.semaphore_signal(barrier, inc=1, device_id=(q, p), device_id_type=MESH)
-        pl.semaphore_wait(barrier, 31)
-
-    @pl.when(p == q)
-    def _():
-        pl.semaphore_wait(barrier, 30)
-
+    pl.semaphore_wait(barrier, 30)
     load.wait()
     out = Sends(send_sem)
 
@@ -166,14 +210,24 @@
                 k = row_of(z, lax.rem(x + i, 4), 1 - c)
                 arrived(buf.at[chunk(k)], sems.at[k], None, (p != 0) if root else None)
 
+    pairs = pc.reshape(2, 8, CH, N)
+    j = x * 2 + c
+    no_root = p != 0
+
+    def pair_send(k, d, cond):
+        out.go(pairs.at[:, k], pairs.at[:, k], pc_sem.at[k], (d, q), cond)
+
+    def pair_wait(k):
+        arrived(pairs.at[:, k], pc_sem.at[k], None, no_root)
+
     lane = lax.broadcasted_iota(jnp.int32, (NB, N), 1)
 
     @pl.when(p == 0)
     def _():
         pc[...] = jnp.where((q == 0) & (lane < NB), 0.0, s[0:NB, :])
 
-    for k in (14, 15, 12, 13, 10, 11, 8, 9, 6, 7, 4, 5, 2, 3, 1):
-        out.go(pc.at[chunk(k)], pc.at[chunk(k)], pc_sem.at[k], (k, q), p == 0)
+    for k in (4, 5, 2, 3, 6, 7, 1):
+        pair_send(k, k, p == 0)
 
     @pl.when(q == 0)
     def _():
@@ -182,15 +236,30 @@
     for k in (15, 14, 13, 12, 11, 10, 9, 8, 7, 6, 5, 4, 3, 2, 1):
         out.go(pr.at[chunk(k)], pr.at[chunk(k)], pr_sem.at[k], (p, k), q == 0)
 
+    near, far = zh == 0, zh == 1
+    pl.when(near & no_root)(lambda: arrived(pairs.at[:, j], pc_sem.at[j], None))
+    pair_send(j, row_of(1, x, c), near)
+
+    def pair_spread(here):
+        for i in (1, 3, 2):
+            d = row_of(zh, lax.rem(x + i, 4), c)
+            pair_send(j, d, here & (d != 0))
+        d = row_of(zh, x, 1 - c)
+        pair_send(j, d, here & (d != 0))
+
+    pair_spread(near)
     arrived(pr.at[chunk(q)], pr_sem.at[q], None, q != 0)
     col_start(pr, pr_sem, True)
-    arrived(pc.at[chunk(p)], pc_sem.at[p], None, p != 0)
-    row_start(pc, pc_sem, True)
+    pl.when(far)(lambda: arrived(pairs.at[:, j], pc_sem.at[j], None))
+    pair_spread(far)
     col_forward(pr, pr_sem, True)
-    row_partner(pc, pc_sem, True)
-    row_own(pc, pc_sem, True, zh)
-    row_own(pc, pc_sem, True, 1 - zh)
-    row_finish(pc, pc_sem, True)
+    for i in (1, 3, 2):
+        k = lax.rem(x + i, 4) * 2 + c
+        pair_wait(k)
+        d = row_of(zh, x, 1 - c)
+        pair_send(k, d, d != 0)
+    for i in (0, 1, 3, 2):
+        pair_wait(lax.rem(x + i, 4) * 2 + 1 - c)
 
     gp[...] = dot3(pc[...], pc[...], LAST)
     grs[pl.ds(q, 1)] = gp[chunk(q), :][None]
@@ -253,16 +322,16 @@
 
     out.go(wp.at[:, 1 - c], r1, r1_sem, (row_of(zh, x, 1 - c), q))
 
+    arrived(r1, r1_sem, None)
+    t[...] = wp[:, pl.ds(c, 1)][:, 0] + r1[...]
+    for phase, z in ((0, 1 - zh), (1, zh)):
+        for i in (1, 3, 2):
+            xx = lax.rem(x + i, 4)
+            out.go(t.at[z * 4 + xx], r2.at[phase, i - 1], r2_sem.at[phase, i - 1], (row_of(zh, xx, c), q))
     wait_slots(grs, grs_sem, q)
     gf[chunk(q), :] = jnp.sum(grs[...], axis=0)
     start_all(gram_all)
 
-    arrived(r1, r1_sem, None)
-    t[...] = wp[:, pl.ds(c, 1)][:, 0] + r1[...]
-    for phase, z in ((0, 1 - zh), (1, zh)):
-        for i in (1, 3, 2):
-            xx = lax.rem(x + i, 4)
-            out.go(t.at[z * 4 + xx], r2.at[phase, i - 1], r2_sem.at[phase, i - 1], (row_of(zh, xx, c), q))
     for i in (1, 3, 2):
         arrived(r2.at[0, i - 1], r2_sem.at[0, i - 1], None)
     u[...] = t[(1 - zh) * 4 + x] + (r2[0, 0] + r2[0, 1] + r2[0, 2])
@@ -274,7 +343,9 @@
     mine = part + r3[...]
     wc[chunk(p), :] = mine
 
-    out.go(wc.at[chunk(p)], wr.at[chunk(p)], wr_sem.at[p], (q, p), p != q)
+    for z in range(4):
+        d = z * 4 + p % 4
+        out.go(wc.at[chunk(p)], wr.at[chunk(p)], wr_sem.at[p], (q, d), (p != q) | (d != q))
 
     @pl.when(p == q)
     def _():
@@ -283,19 +354,61 @@
     row_start(wc, wc_sem, False)
     crs[pl.ds(q, 1)] = dot3(mine, pc[...], LAST)[None]
     start_all(curv_copy)
-    arrived(wr.at[chunk(q)], wr_sem.at[q], None, p != q)
-    col_start(wr, wr_sem, False)
+    wait_chunks(gf, gf_sem, q)
+    row = lax.broadcasted_iota(jnp.int32, (NB, NB), 0)
+    col = lax.broadcasted_iota(jnp.int32, (NB, NB), 1)
+    aug[:, 0:NB] = gf[...]
+    aug[:, NB:] = (row == col).astype(F32)
+    factor_block(aug, 0)
+    for i in range(4):
+        k = lax.rem(zl + i, 4) * 4 + y
+        arrived(wr.at[chunk(k)], wr_sem.at[k], None, (p != q) | (k != q))
+        for n in (1, 3, 2):
+            d = zl * 4 + lax.rem(y + n, 4)
+            out.go(wr.at[chunk(k)], wr.at[chunk(k)], wr_sem.at[k], (p, d))
     row_partner(wc, wc_sem, False)
+    factor_block(aug, 1)
     row_own(wc, wc_sem, False, zh)
-    col_forward(wr, wr_sem, False)
     wait_slots(crs, crs_sem, q)
     cf[chunk(p), :] = jnp.sum(crs[...], axis=0)
     start_all(curv_all)
+    factor_block(aug, 2)
     row_own(wc, wc_sem, False, 1 - zh)
+    factor_block(aug, 3)
+    rfac[...] = jnp.where(row <= col, aug[:, 0:NB], 0.0)
+    inverse = aug[:, NB:]
+    m = split(2.0 * dot6(inverse, inverse, FIRST))
+    ar[...] = dot3s(m, split(pr[...]), PLAIN)
+    ac[...] = dot3s(m, split(pc[...]), PLAIN)
+
+    def put(ref, blocks, axis):
+        for i, block in enumerate(blocks):
+            here = slice(i * NB, (i + 1) * NB)
+            if axis == 0:
+                ref[here, :] = block
+            else:
+                ref[:, here] = block
+
+    ah, al = split(ar[...].T)
+    put(left.at[:, 0:NB], (ah,), 1)
+    put(left.at[:, 2 * NB : 3 * NB], (ah,), 1)
+    put(left.at[:, 4 * NB : 5 * NB], (al,), 1)
+    ah, al = split(ac[...])
+    put(right.at[NB : 2 * NB], (ah,), 0)
+    put(right.at[3 * NB : 4 * NB], (al,), 0)
+    put(right.at[5 * NB : 6 * NB], (ah,), 0)
+    wait_chunks(cf, cf_sem, p)
+    half = split(0.5 * cf[...])
     row_finish(wc, wc_sem, False)
-    wait_chunks(gf, gf_sem, q)
-    wait_chunks(cf, cf_sem, p)
+    vh, vl = split(wc[...] - dot3s(half, split(ac[...]), PLAIN))
+    put(right.at[0:NB], (vh,), 0)
+    put(right.at[2 * NB : 3 * NB], (vl,), 0)
+    put(right.at[4 * NB : 5 * NB], (vh,), 0)
     col_finish(wr, wr_sem, False)
+    vh, vl = split((wr[...] - dot3s(half, split(ar[...]), PLAIN)).T)
+    put(left.at[:, NB : 2 * NB], (vh,), 1)
+    put(left.at[:, 3 * NB : 4 * NB], (vh,), 1)
+    put(left.at[:, 5 * NB : 6 * NB], (vl,), 1)
     out.drain()
     for make in (gram_copy, gram_all, curv_copy, curv_all):
         drain_all(make)
@@ -304,14 +417,19 @@
 def exchange(matrix):
     vm = pl.BlockSpec(memory_space=pltpu.VMEM)
     dma = pltpu.SemaphoreType.DMA
-    big = jax.ShapeDtypeStruct((NB, N), F32)
-    small = jax.ShapeDtypeStruct((NB, NB), F32)
+    big = pltpu.VMEM((NB, N), F32)
+    small = pltpu.VMEM((NB, NB), F32)
     return pl.pallas_call(
         exchange_kernel,
-        out_shape=(big, big, big, big, small, small),
-        in_specs=[pl.BlockSpec(memory_space=pl.ANY)],
-        out_specs=(vm,) * 6,
+        out_shape=(
+            jax.ShapeDtypeStruct((N, 6 * NB), BF16),
+            jax.ShapeDtypeStruct((6 * NB, N), BF16),
+            jax.ShapeDtypeStruct((NB, NB), F32),
+        ),
+        in_specs=[pl.BlockSpec(memory_space=pltpu.HBM)],
+        out_specs=(vm,) * 3,
         scratch_shapes=[
+            big, big, big, big, small, small,
             pltpu.VMEM((N, N), F32),
             pltpu.VMEM((8, 2, CH, N), F32),
             pltpu.VMEM((8, CH, N), F32),
@@ -319,70 +437,20 @@
             pltpu.VMEM((2, 3, CH, N), F32),
             pltpu.VMEM((CH, N), F32),
             pltpu.VMEM((CH, N), F32),
-            pltpu.VMEM((NB, NB), F32),
+            small,
             pltpu.VMEM((16, CH, NB), F32),
             pltpu.VMEM((16, CH, NB), F32),
+            pltpu.VMEM((NB, 2 * NB), F32),
+            big, big,
             dma, dma((128,)), dma((16,)), dma((16,)), dma((16,)), dma((16,)),
-            dma((16,)), dma((16,)), dma((16,)), dma((16,)), dma, dma((2, 3)), dma, dma((16,)), dma((16,)), dma((16,)), dma((16,)),
+            dma((16,)), dma((8,)), dma((16,)), dma((16,)), dma, dma((2, 3)), dma, dma((16,)), dma((16,)), dma((16,)), dma((16,)),
         ],
         compiler_params=pltpu.CompilerParams(collective_id=0, has_side_effects=True, vmem_limit_bytes=40 << 20),
         name="exchange",
     )(matrix)
 
 
-def factor(aug):
-    b = 64
-    row = lax.broadcasted_iota(jnp.int32, (b, 2 * b), 0)
-    col = lax.broadcasted_iota(jnp.int32, (b, 2 * b), 1)
-    eye = (row + b == col).astype(F32)
-    for k in range(4):
-        here = slice(k * b, (k + 1) * b)
-        a = jnp.concatenate([aug[here, here], eye[:, b:]], axis=1)
-        for j in range(0, b, 2):
-            c0, c1 = a[:, j : j + 1], a[:, j + 1 : j + 2]
-            r0, r1 = a[j : j + 1, :], a[j + 1 : j + 2, :]
-            a00, a01, a11 = a[j : j + 1, j : j + 1], a[j : j + 1, j + 1 : j + 2], a[j + 1 : j + 2, j + 1 : j + 2]
-            inv = 1.0 / (a00 * a11 - a01 * a01)
-            w0 = (a11 * r0 - a01 * r1) * inv
-            w1 = (a00 * r1 - a01 * r0) * inv
-            rest = c0 * w0 + c1 * w1
-            second = (a01 / a00) * r0
-            a = a - jnp.where(row > j + 1, rest, jnp.where(row == j + 1, second, 0.0))
-        diag = jnp.sum(jnp.where(row == col, a, 0.0), axis=1, keepdims=True)
-        inverse = (a * lax.rsqrt(diag))[:, b:]
-        done = dot6(inverse, aug[here, :], PLAIN)
-        aug[here, :] = done
-        if k < 3:
-            below = slice((k + 1) * b, NB)
-            aug[below, :] = aug[below, :] - dot6(done[:, 0:NB], done, FIRST)[below, :]
-
-
-def finish_kernel(pr, pc, wr, wc, gf, cf, s, out, r, aug, left, right):
-    @pl.when(pl.program_id(0) == 0)
-    def _():
-        row = lax.broadcasted_iota(jnp.int32, (NB, NB), 0)
-        col = lax.broadcasted_iota(jnp.int32, (NB, NB), 1)
-        aug[:, 0:NB] = gf[...]
-        aug[:, NB:] = (row == col).astype(F32)
-        factor(aug)
-        r[...] = jnp.where(row <= col, aug[:, 0:NB], 0.0)
-        inverse = aug[:, NB:]
-        m = split(2.0 * dot6(inverse, inverse, FIRST))
-        half = split(0.5 * cf[...])
-        for panel, image, side in ((pr, wr, 0), (pc, wc, 1)):
-            a = dot3s(m, split(panel[...]), PLAIN)
-            v = image[...] - dot3s(half, split(a), PLAIN)
-            if side == 0:
-                ah, al = split(a.T)
-                vh, vl = split(v.T)
-                for i, block in enumerate((ah, vh, ah, vh, al, vl)):
-                    left[:, i * NB : (i + 1) * NB] = block
-            else:
-                ah, al = split(a)
-                vh, vl = split(v)
-                for i, block in enumerate((vh, ah, vl, al, vh, ah)):
-                    right[i * NB : (i + 1) * NB, :] = block
-
+def finish_kernel(left, right, s, out):
     rows = pl.ds(pl.multiple_of(pl.program_id(0) * TILE, TILE), TILE)
     out[...] = s[...] - dot(left[rows, :], right[...], PLAIN)
 
@@ -390,23 +458,23 @@
 TILE = 128
 
 
-def finish(parts, matrix):
-    whole = lambda shape: pl.BlockSpec(shape, lambda i: (0, 0))
-    big, small, tile = whole((NB, N)), whole((NB, NB)), pl.BlockSpec((TILE, N), lambda i: (i, 0))
+def finish(left, right, matrix):
+    whole = lambda a: pl.BlockSpec(a.shape, lambda i: (0, 0))
+    tile = pl.BlockSpec((TILE, N), lambda i: (i, 0))
     return pl.pallas_call(
         finish_kernel,
         grid=(N // TILE,),
-        out_shape=(jax.ShapeDtypeStruct((N, N), F32), jax.ShapeDtypeStruct((NB, NB), F32)),
-        in_specs=[big, big, big, big, small, small, tile],
-        out_specs=(tile, small),
-        scratch_shapes=[pltpu.VMEM((NB, 2 * NB), F32), pltpu.VMEM((N, 6 * NB), BF16), pltpu.VMEM((6 * NB, N), BF16)],
-        compiler_params=pltpu.CompilerParams(vmem_limit_bytes=48 << 20),
+        out_shape=jax.ShapeDtypeStruct((N, N), F32),
+        in_specs=[whole(left), whole(right), tile],
+        out_specs=tile,
+        compiler_params=pltpu.CompilerParams(vmem_limit_bytes=32 << 20),
         name="finish",
-    )(*parts, matrix)
+    )(left, right, matrix)
 
 
 def on_device(matrix):
-    return finish(exchange(matrix), matrix)
+    left, right, factor = exchange(matrix)
+    return finish(left, right, matrix), factor
 
 
 def solution(mesh):

time: 137 us -> 105 us (0.77)
  the two profiles are of different devices: /device:TPU:32 before, /device:TPU:1 now
where the time goes in v2:
time: 105 us; the launch traced here: 104 us
  Pallas kernels  101 us (96%)
  local copies, waits for them, and re-layouts  2.89 us (3%)
    pallas_call x1, Pallas kernels, exchange(): pl.pallas_call(exchange_kernel, out_shape=(jax.ShapeDtypeStruct((N, 6 * N...  94.4 us
    pallas_call x1, Pallas kernels, finish(): pl.pallas_call(finish_kernel, grid=(N // TILE,), out_shape=jax.ShapeDtype...  6.18 us
    unnamed x5, local copies, waits for them, and re-layouts  2.89 us

profile of v2, /device:TPU:1, one launch (start us, length us, event | category | flops | bytes accessed | tf_op | source)
XLA Modules:
  0.0 104.1 jit_solution(885186097851788357)
XLA Ops:
  0.6 0.0 copy-start
  0.6 2.2 %copy-done = f32[1024,1024]{1,0:T(8,128)S(1)} copy-done((f32[1024,1024]{1,0:T(8,128)S(1)}, f32[1024,1024]{1,0:T(8,128)}, u32[]{:S(2)}) %copy-start) | copy-done | bytes 4194328
  2.8 0.0 copy-start.1
  2.8 94.4 %exchange.1 = (bf16[1024,1536]{1,0:T(8,128)(2,1)S(1)}, bf16[1536,1024]{1,0:T(8,128)(2,1)S(1)}, f32[256,256]{1,0:T(8,128)S(1)}) custom-call(f32[1024,1024]{1,0:T(8,128)S(1)} %copy-done), custom_call_target="tpu_custom_call" | custom-call | tf_op jit(solution)/shard_map/exchange/pallas_call | solution.py:422
  97.2 0.0 copy-done.1
  97.2 6.2 %finish.1 = f32[1024,1024]{1,0:T(8,128)} custom-call(bf16[1024,1536]{1,0:T(8,128)(2,1)S(1)} %get-tuple-element.5.left, bf16[1536,1024]{1,0:T(8,128)(2,1)S(1)} %get-tuple-element.6.right, f32[1024,1024]{1,0:T(8,128)S(1)} %copy-done.1), custom_call_target="tpu_custom_call" | custom-call | tf_op jit(solution)/shard_map/finish/pallas_call | solution.py:464
  103.4 0.7 copy.4
Async XLA Ops:
  0.6 2.2 %copy-start = (f32[1024,1024]{1,0:T(8,128)S(1)}, f32[1024,1024]{1,0:T(8,128)}, u32[]{:S(2)}) copy-start(f32[1024,1024]{1,0:T(8,128)} %s.1) | copy-start | bytes 12582916
  2.8 94.4 %copy-start.1 = (f32[1024,1024]{1,0:T(8,128)S(1)}, f32[1024,1024]{1,0:T(8,128)}, u32[]{:S(2)}) copy-start(f32[1024,1024]{1,0:T(8,128)} %s.1) | copy-start | bytes 12582916

commit v3 on v2

v3 whole, which is shorter than its diff:
```python
import functools
import jax
import jax.numpy as jnp
from jax import lax
from jax.experimental import pallas as pl
from jax.experimental.pallas import tpu as pltpu
from jax.sharding import PartitionSpec as P

NB = 256
N = 1024
CH = 16
MESH = pl.DeviceIdType.MESH
F32 = jnp.float32
BF16 = jnp.bfloat16

LAST = (((1,), (1,)), ((), ()))
FIRST = (((0,), (0,)), ((), ()))
PLAIN = (((1,), (0,)), ((), ()))


def split(x):
    hi = x.astype(BF16)
    lo = (x - hi.astype(F32)).astype(BF16)
    return hi, lo


def dot(a, b, dims):
    return lax.dot_general(a, b, dims, preferred_element_type=F32)


def dot3s(a, b, dims):
    (ah, al), (bh, bl) = a, b
    return dot(ah, bh, dims) + (dot(ah, bl, dims) + dot(al, bh, dims))


def dot3(a, b, dims):
    return dot3s(split(a), split(b), dims)


def dot6(a, b, dims):
    return lax.dot_general(a, b, dims, precision=lax.Precision.HIGHEST, preferred_element_type=F32)


def chunk(k):
    return pl.ds(pl.multiple_of(k * CH, CH), CH)


class Sends:
    def __init__(self, sems):
        self.sems = sems
        self.count = 0
        self.pending = []

    def go(self, src, dst, recv, dev, cond=None):
        copy = pltpu.make_async_remote_copy(
            src_ref=src, dst_ref=dst, send_sem=self.sems.at[self.count], recv_sem=recv, device_id=dev, device_id_type=MESH
        )
        self.count += 1
        self.pending.append((copy, cond))
        when(cond, copy.start)

    def drain(self):
        for copy, cond in self.pending:
            when(cond, copy.wait_send)
        self.pending = []


def when(cond, fn):
    if cond is None:
        fn()
    else:
        pl.when(cond)(fn)


def arrived(ref, recv, cond=None):
    copy = pltpu.make_async_copy(ref, ref, recv)
    when(cond, copy.wait)


def reciprocal(x):
    y = pl.reciprocal(x, approx=True)
    return y * (2.0 - x * y)


def pivot8(step, a):
    tiles = [a[8 * t : 8 * t + 8, :] for t in range(8)]
    sub = lax.broadcasted_iota(jnp.int32, (8, 128), 0)
    full = lambda v: jnp.broadcast_to(v, (8, 128))
    cols = [[full(tile[:, i : i + 1]) for i in range(8)] for tile in tiles]
    e = [[full(cols[0][k][i : i + 1, :]) if k >= i else None for k in range(8)] for i in range(8)]
    rows = [full(tiles[0][i : i + 1, :]) for i in range(8)]
    scaled = []
    for i in range(8):
        inv = reciprocal(e[i][i])
        scaled.append(rows[i] * inv)
        for k in range(i + 1, 8):
            f = e[i][k] * inv
            rows[k] = rows[k] - f * rows[i]
            for n in range(k, 8):
                e[k][n] = e[k][n] - f * e[i][n]
            for t in range(1, 8):
                cols[t][k] = cols[t][k] - cols[t][i] * f
    top = rows[0]
    for i in range(1, 8):
        top = jnp.where(sub == i, rows[i], top)
    new = []
    for t in range(1, 8):
        term = cols[t][0] * scaled[0]
        for i in range(1, 8):
            term = term + cols[t][i] * scaled[i]
        new.append(tiles[t] - term * jnp.where(step + t < 8, 1.0, 0.0).astype(F32))
    return pltpu.roll(jnp.concatenate(new + [top], axis=0), 120, axis=1)


def factor_block(aug, k):
    b = 64
    row = lax.broadcasted_iota(jnp.int32, (b, 2 * b), 0)
    col = lax.broadcasted_iota(jnp.int32, (b, 2 * b), 1)
    here = slice(k * b, (k + 1) * b)
    eye = (row + b == col).astype(F32)
    a = jnp.concatenate([aug[here, here], eye[:, b:]], axis=1)
    a = lax.fori_loop(0, 8, pivot8, a)
    diag = jnp.sum(jnp.where(row + b == col, a, 0.0), axis=1, keepdims=True)
    inverse = (a * lax.rsqrt(diag))[:, :b]
    done = dot6(inverse, aug[here, :], PLAIN)
    aug[here, :] = done
    if k < 3:
        below = slice((k + 1) * b, NB)
        aug[below, :] = aug[below, :] - dot6(done[:, (k + 1) * b : NB], done, FIRST)


def exchange_kernel(
    s_hbm, left, right, rfac,
    pr, pc, wr, wc, gf, cf, s, wp, r1, t, r2, u, r3, gp, grs, crs, aug, ac,
    load_sem, send_sem, gsend, gasend, csend, casend,
    pr_sem, pc_sem, wr_sem, wc_sem, r1_sem, r2_sem, r3_sem, grs_sem, gf_sem, crs_sem, cf_sem,
):
    p = lax.axis_index("row")
    q = lax.axis_index("col")
    zh, x, c = p // 8, (p // 2) % 4, p % 2
    zl, y = q // 4, q % 4
    same = p == q
    j = x * 2 + c

    load = pltpu.make_async_copy(s_hbm, s, load_sem)
    load.start()

    barrier = pltpu.get_barrier_semaphore()

    def hello(dev):
        pl.semaphore_signal(barrier, inc=1, device_id=dev, device_id_type=MESH)

    def greet(i, carry):
        hello((lax.rem(p + i, 16), q))
        hello((p, lax.rem(q + i, 16)))
        return carry

    lax.fori_loop(1, 16, greet, 0)
    pl.semaphore_wait(barrier, 30)
    load.wait()
    out = Sends(send_sem)

    def send_chunk(buf, sems, k, dev, cond=None):
        out.go(buf.at[chunk(k)], buf.at[chunk(k)], sems.at[k], dev, cond)

    def wait_chunk(buf, sems, k, cond=None):
        arrived(buf.at[chunk(k)], sems.at[k], cond)


    def col_of(i, n):
        return lax.rem(zl + i, 4) * 4 + lax.rem(y + n, 4)

    def col_z(buf, sems, root):
        for i in (1, 3, 2):
            d = col_of(i, 0)
            send_chunk(buf, sems, q, (p, d), (d != 0) if root else None)

    def col_y(buf, sems, root, i):
        k = col_of(i, 0)
        if i:
            wait_chunk(buf, sems, k, (q != 0) if root else None)
        for n in (1, 3, 2):
            d = col_of(0, n)
            send_chunk(buf, sems, k, (p, d), (d != 0) if root else None)

    def col_finish(buf, sems, root):
        for i in (0, 1, 3, 2):
            for n in (1, 3, 2):
                wait_chunk(buf, sems, col_of(i, n), (q != 0) if root else None)


    def pair_send(buf, sems, k, d, cond):
        view = buf.reshape(2, 8, CH, N)
        out.go(view.at[:, k], view.at[:, k], sems.at[k], (d, q), cond)

    def pair_wait(buf, sems, k, cond):
        arrived(buf.reshape(2, 8, CH, N).at[:, k], sems.at[k], cond)

    def pair_spread(buf, sems, here):
        for i in (1, 3, 2):
            d = zh * 8 + lax.rem(x + i, 4) * 2 + c
            pair_send(buf, sems, j, d, here & (d != 0))
        d = zh * 8 + x * 2 + 1 - c
        pair_send(buf, sems, j, d, here & (d != 0))

    def pair_forward(buf, sems, root):
        d = zh * 8 + x * 2 + 1 - c
        for i in (1, 3, 2):
            k = lax.rem(x + i, 4) * 2 + c
            pair_wait(buf, sems, k, (p != 0) if root else None)
            pair_send(buf, sems, k, d, (d != 0) if root else None)

    def pair_finish(buf, sems, root):
        for i in (0, 1, 3, 2):
            pair_wait(buf, sems, lax.rem(x + i, 4) * 2 + 1 - c, (p != 0) if root else None)


    def row_of(z, i, core):
        return z * 8 + lax.rem(x + i, 4) * 2 + core

    def row_spread(buf, sems, k):
        for i in (1, 3, 2):
            send_chunk(buf, sems, k, (row_of(zh, i, c), q))
        send_chunk(buf, sems, k, (row_of(zh, 0, 1 - c), q))

    def row_start(buf, sems):
        send_chunk(buf, sems, p, (row_of(1 - zh, 0, c), q))
        row_spread(buf, sems, p)

    def row_partner(buf, sems):
        k = row_of(1 - zh, 0, c)
        wait_chunk(buf, sems, k)
        row_spread(buf, sems, k)

    def row_own(buf, sems, z):
        for i in (1, 3, 2):
            k = row_of(z, i, c)
            wait_chunk(buf, sems, k)
            send_chunk(buf, sems, k, (row_of(zh, 0, 1 - c), q))

    def row_finish(buf, sems):
        for z in (zh, 1 - zh):
            for i in (0, 1, 3, 2):
                wait_chunk(buf, sems, row_of(z, i, 1 - c))


    def direct(src, dst, ssem, rsem, dev):
        return pltpu.make_async_remote_copy(
            src_ref=src, dst_ref=dst, send_sem=ssem, recv_sem=rsem, device_id=dev, device_id_type=MESH
        )

    def gram_copy(i):
        d = lax.rem(q + i, 16)
        return direct(gp.at[chunk(d)], grs.at[q], gsend.at[i], grs_sem.at[q], (p, d))

    def gram_all(i):
        d = lax.rem(q + i, 16)
        return direct(gf.at[chunk(q)], gf.at[chunk(q)], gasend.at[i], gf_sem.at[q], (p, d))

    def curv_copy(i):
        d = lax.rem(q + i, 16)
        return direct(crs.at[q], crs.at[q], csend.at[i], crs_sem.at[q], (p, d))

    def curv_all(i):
        d = lax.rem(p + i, 16)
        return direct(cf.at[chunk(p)], cf.at[chunk(p)], casend.at[i], cf_sem.at[p], (d, q))

    def start_all(make):
        lax.fori_loop(1, 16, lambda i, z: (make(i).start(), z)[1], 0)

    def drain_all(make):
        lax.fori_loop(1, 16, lambda i, z: (make(i).wait_send(), z)[1], 0)

    def wait_slots(buf, sems, me):
        def step(i, z):
            k = lax.rem(me + i, 16)
            arrived(buf.at[k], sems.at[k])
            return z

        lax.fori_loop(1, 16, step, 0)

    def wait_chunks(buf, sems, me):
        def step(i, z):
            wait_chunk(buf, sems, lax.rem(me + i, 16))
            return z

        lax.fori_loop(1, 16, step, 0)

    lane = lax.broadcasted_iota(jnp.int32, (NB, N), 1)

    @pl.when(p == 0)
    def _():
        pc[...] = jnp.where((q == 0) & (lane < NB), 0.0, s[0:NB, :])

    for k in (4, 5, 2, 3, 6, 7, 1):
        pair_send(pc, pc_sem, k, k, p == 0)

    @pl.when(q == 0)
    def _():
        pr[...] = jnp.where((p == 0) & (lane < NB), 0.0, s[:, 0:NB].T)

    for i in range(4):
        for n in (1, 3, 2):
            send_chunk(pr, pr_sem, i * 4 + n, (p, n), q == 0)

    def line(i, here):
        k = i * 4 + y
        wait_chunk(pr, pr_sem, k, here & (q != 0))
        send_chunk(pr, pr_sem, k, (p, lax.rem(q + 4, 16)), here & (zl < 3))
        for n in (1, 3, 2):
            d = col_of(0, n)
            send_chunk(pr, pr_sem, k, (p, d), here & (d != 0))

    near, far, first = zh == 0, zh == 1, zl == 0
    line(0, first)
    pair_wait(pc, pc_sem, j, near & (p != 0))
    pair_send(pc, pc_sem, j, 8 + j, near)
    pair_spread(pc, pc_sem, near)
    line(0, zl > 0)
    line(1, zl >= 0)
    pair_wait(pc, pc_sem, j, far)
    pair_spread(pc, pc_sem, far)
    line(2, zl >= 0)
    line(3, zl >= 0)
    pair_forward(pc, pc_sem, True)
    pair_finish(pc, pc_sem, True)

    pch, pcl = split(pc[...])
    gp[...] = dot3s((pch, pcl), (pch, pcl), LAST)
    grs[pl.ds(q, 1)] = gp[chunk(q), :][None]
    start_all(gram_copy)

    col_finish(pr, pr_sem, True)
    prh, prl = split(pr[...])

    def product(i, z):
        cols = pl.ds(pl.multiple_of(i * 256, 256), 256)
        wp.reshape(NB, N)[:, cols] = dot3s((prh, prl), split(s[:, cols]), PLAIN)
        return z

    lax.fori_loop(0, 4, product, 0)

    out.go(wp.at[:, 1 - c], r1, r1_sem, (zh * 8 + x * 2 + 1 - c, q))
    wait_slots(grs, grs_sem, q)
    gf[chunk(q), :] = jnp.sum(grs[...], axis=0)
    start_all(gram_all)
    arrived(r1, r1_sem)
    t[...] = wp[:, pl.ds(c, 1)][:, 0] + r1[...]
    for phase, z in ((0, 1 - zh), (1, zh)):
        for i in (1, 3, 2):
            xx = lax.rem(x + i, 4)
            out.go(t.at[z * 4 + xx], r2.at[phase, i - 1], r2_sem.at[phase, i - 1], (zh * 8 + xx * 2 + c, q))
    for i in (1, 3, 2):
        arrived(r2.at[0, i - 1], r2_sem.at[0, i - 1])
    u[...] = t[(1 - zh) * 4 + x] + (r2[0, 0] + r2[0, 1] + r2[0, 2])
    out.go(u, r3, r3_sem, ((1 - zh) * 8 + j, q))
    wait_chunks(gf, gf_sem, q)
    row = lax.broadcasted_iota(jnp.int32, (NB, NB), 0)
    col = lax.broadcasted_iota(jnp.int32, (NB, NB), 1)
    aug[:, 0:NB] = gf[...]
    aug[:, NB:] = (row == col).astype(F32)
    factor_block(aug, 0)
    for i in (1, 3, 2):
        arrived(r2.at[1, i - 1], r2_sem.at[1, i - 1])
    part = t[zh * 4 + x] + (r2[1, 0] + r2[1, 1] + r2[1, 2])
    arrived(r3, r3_sem)
    mine = part + r3[...]
    wc[chunk(p), :] = mine

    out.go(wc.at[chunk(p)], wr.at[chunk(p)], wr_sem.at[p], (q, p), p != q)
    row_start(wc, wc_sem)

    @pl.when(same)
    def _():
        wr[chunk(q), :] = mine

    crs[pl.ds(q, 1)] = dot3s(split(mine), (pch, pcl), LAST)[None]
    start_all(curv_copy)
    factor_block(aug, 1)
    wait_chunk(wr, wr_sem, q, p != q)
    col_z(wr, wr_sem, False)
    col_y(wr, wr_sem, False, 0)
    row_partner(wc, wc_sem)
    factor_block(aug, 2)
    for i in (1, 3, 2):
        col_y(wr, wr_sem, False, i)
    row_own(wc, wc_sem, zh)
    wait_slots(crs, crs_sem, q)
    cf[chunk(p), :] = jnp.sum(crs[...], axis=0)
    start_all(curv_all)
    factor_block(aug, 3)
    row_own(wc, wc_sem, 1 - zh)
    rfac[...] = jnp.where(row <= col, aug[:, 0:NB], 0.0)
    inverse = aug[:, NB:]
    m = split(2.0 * dot6(inverse, inverse, FIRST))
    ac[...] = dot3s(m, split(pc[...]), PLAIN)
    ah, al = split(ac[...])
    right[NB : 2 * NB, :] = ah
    right[3 * NB : 4 * NB, :] = al
    rh, rl = split(dot3s(m, split(pr[...]), PLAIN).T)
    left[:, 0:NB] = rh
    left[:, 2 * NB : 3 * NB] = rl

    wait_chunks(cf, cf_sem, p)
    turned = dot3s(split(cf[...]), (ah, al), PLAIN)
    row_finish(wc, wc_sem)
    vh, vl = split(wc[...] - turned)
    right[0:NB, :] = vh
    right[2 * NB : 3 * NB, :] = vl
    col_finish(wr, wr_sem, False)
    vh, vl = split(wr[...].T)
    left[:, NB : 2 * NB] = vh
    left[:, 3 * NB : 4 * NB] = vl
    out.drain()
    for make in (gram_copy, gram_all, curv_copy, curv_all):
        drain_all(make)


def exchange(matrix):
    vm = pl.BlockSpec(memory_space=pltpu.VMEM)
    dma = pltpu.SemaphoreType.DMA
    big = pltpu.VMEM((NB, N), F32)
    small = pltpu.VMEM((NB, NB), F32)
    return pl.pallas_call(
        exchange_kernel,
        out_shape=(
            jax.ShapeDtypeStruct((N, 4 * NB), BF16),
            jax.ShapeDtypeStruct((4 * NB, N), BF16),
            jax.ShapeDtypeStruct((NB, NB), F32),
        ),
        in_specs=[pl.BlockSpec(memory_space=pltpu.HBM)],
        out_specs=(vm,) * 3,
        scratch_shapes=[
            big, big, big, big, small, small,
            pltpu.VMEM((N, N), F32),
            pltpu.VMEM((8, 2, CH, N), F32),
            pltpu.VMEM((8, CH, N), F32),
            pltpu.VMEM((8, CH, N), F32),
            pltpu.VMEM((2, 3, CH, N), F32),
            pltpu.VMEM((CH, N), F32),
            pltpu.VMEM((CH, N), F32),
            small,
            pltpu.VMEM((16, CH, NB), F32),
            pltpu.VMEM((16, CH, NB), F32),
            pltpu.VMEM((NB, 2 * NB), F32),
            big,
            dma, dma((96,)), dma((16,)), dma((16,)), dma((16,)), dma((16,)),
            dma((16,)), dma((8,)), dma((16,)), dma((16,)), dma, dma((2, 3)), dma,
            dma((16,)), dma((16,)), dma((16,)), dma((16,)),
        ],
        compiler_params=pltpu.CompilerParams(collective_id=0, has_side_effects=True, vmem_limit_bytes=48 << 20),
        name="exchange",
    )(matrix)


def finish_kernel(left, right, factor, s, out, r):
    rows = pl.ds(pl.multiple_of(pl.program_id(0) * TILE, TILE), TILE)
    half = 2 * NB
    lh, ll = left[rows, 0:half], left[rows, half:]
    rh, rl = right[0:half, :], right[half:, :]
    out[...] = s[...] - (dot(lh, rh, PLAIN) + (dot(lh, rl, PLAIN) + dot(ll, rh, PLAIN)))
    r[...] = factor[...]


TILE = 128


def finish(left, right, factor, matrix):
    whole = lambda a: pl.BlockSpec(a.shape, lambda i: (0, 0))
    tile = pl.BlockSpec((TILE, N), lambda i: (i, 0))
    return pl.pallas_call(
        finish_kernel,
        grid=(N // TILE,),
        out_shape=(jax.ShapeDtypeStruct((N, N), F32), jax.ShapeDtypeStruct((NB, NB), F32)),
        in_specs=[whole(left), whole(right), whole(factor), tile],
        out_specs=(tile, whole(factor)),
        compiler_params=pltpu.CompilerParams(vmem_limit_bytes=32 << 20),
        name="finish",
    )(left, right, factor, matrix)


def on_device(matrix):
    return finish(*exchange(matrix), matrix)


def solution(mesh):
    return jax.shard_map(
        on_device,
        mesh=mesh,
        in_specs=(P("row", "col"),),
        out_specs=(P("row", "col"), P()),
        check_vma=False,
    )
```

time: 105 us -> 102 us (0.971)
  the two profiles are of different devices: /device:TPU:1 before, /device:TPU:127 now
where the time goes in v3:
time: 102 us
  Pallas kernels  101 us (99%)
    pallas_call x1, Pallas kernels, exchange(): pl.pallas_call(exchange_kernel, out_shape=(jax.ShapeDtypeStruct((N, 4 * N...  95.2 us
    pallas_call x1, Pallas kernels, finish(): pl.pallas_call(finish_kernel, grid=(N // TILE,), out_shape=(jax.ShapeDtyp...  6.19 us

profile of v3, /device:TPU:127, one launch (start us, length us, event | category | flops | bytes accessed | tf_op | source)
XLA Modules:
  0.0 102.1 jit_solution(2533330594556482241)
XLA Ops:
  0.6 0.0 copy-start
  0.6 95.2 %exchange.1 = (bf16[1024,1024]{1,0:T(8,128)(2,1)S(1)}, bf16[1024,1024]{1,0:T(8,128)(2,1)S(1)}, f32[256,256]{1,0:T(8,128)S(1)}) custom-call(f32[1024,1024]{1,0:T(8,128)} %s.1), custom_call_target="tpu_custom_call" | custom-call | tf_op jit(solution)/shard_map/exchange/pallas_call | solution.py:424
  95.9 0.0 copy-done
  95.9 6.2 %finish.1 = (f32[1024,1024]{1,0:T(8,128)}, f32[256,256]{1,0:T(8,128)}) custom-call(bf16[1024,1024]{1,0:T(8,128)(2,1)S(1)} %get-tuple-element.5.left, bf16[1024,1024]{1,0:T(8,128)(2,1)S(1)} %get-tuple-element.6.right, f32[256,256]{1,0:T(8,128)S(1)} %get-tuple-element.7.factor, f32[1024,1024]{1,0:T(8,128)S(1)} %copy-done), custom_call_target="tpu_custom_call" | custom-call | tf_op jit(solution)/shard_map/finish/pallas_call | solution.py:471
Async XLA Ops:
  0.6 95.3 %copy-start = (f32[1024,1024]{1,0:T(8,128)S(1)}, f32[1024,1024]{1,0:T(8,128)}, u32[]{:S(2)}) copy-start(f32[1024,1024]{1,0:T(8,128)} %s.1) | copy-start | bytes 12582916

commit v4 on v3

--- a/solution.py
+++ b/solution.py
@@ -131,9 +131,9 @@
 
 def exchange_kernel(
     s_hbm, left, right, rfac,
-    pr, pc, wr, wc, gf, cf, s, wp, r1, t, r2, u, r3, gp, grs, crs, aug, ac,
-    load_sem, send_sem, gsend, gasend, csend, casend,
-    pr_sem, pc_sem, wr_sem, wc_sem, r1_sem, r2_sem, r3_sem, grs_sem, gf_sem, crs_sem, cf_sem,
+    pr, pc, wr, wc, gf, cf, s, wp, r1, t, r2, u, r3, gp, grs, c0, c1, cy, cz, aug, ac,
+    load_sem, send_sem, gsend, gdsend, gasend,
+    pr_sem, pc_sem, wr_sem, wc_sem, r1_sem, r2_sem, r3_sem, grs_sem, gf_sem, cy_sem, cz_sem, cf_sem,
 ):
     p = lax.axis_index("row")
     q = lax.axis_index("col")
@@ -257,13 +257,8 @@
         d = lax.rem(q + i, 16)
         return direct(gf.at[chunk(q)], gf.at[chunk(q)], gasend.at[i], gf_sem.at[q], (p, d))
 
-    def curv_copy(i):
-        d = lax.rem(q + i, 16)
-        return direct(crs.at[q], crs.at[q], csend.at[i], crs_sem.at[q], (p, d))
-
-    def curv_all(i):
-        d = lax.rem(p + i, 16)
-        return direct(cf.at[chunk(p)], cf.at[chunk(p)], casend.at[i], cf_sem.at[p], (d, q))
+    def gram_down(i):
+        return direct(gf.at[chunk(q)], gf.at[chunk(q)], gdsend.at[i], gf_sem.at[q], (i, q))
 
     def start_all(make):
         lax.fori_loop(1, 16, lambda i, z: (make(i).start(), z)[1], 0)
@@ -294,6 +289,13 @@
 
     for k in (4, 5, 2, 3, 6, 7, 1):
         pair_send(pc, pc_sem, k, k, p == 0)
+
+    @pl.when(p == 0)
+    def _():
+        both = split(pc[...])
+        gp[...] = dot3s(both, both, LAST)
+        grs[pl.ds(q, 1)] = gp[chunk(q), :][None]
+        start_all(gram_copy)
 
     @pl.when(q == 0)
     def _():
@@ -318,17 +320,21 @@
     pair_spread(pc, pc_sem, near)
     line(0, zl > 0)
     line(1, zl >= 0)
+
+    @pl.when(p == 0)
+    def _():
+        wait_slots(grs, grs_sem, q)
+        gf[chunk(q), :] = jnp.sum(grs[...], axis=0)
+        start_all(gram_down)
+
     pair_wait(pc, pc_sem, j, far)
     pair_spread(pc, pc_sem, far)
     line(2, zl >= 0)
     line(3, zl >= 0)
     pair_forward(pc, pc_sem, True)
     pair_finish(pc, pc_sem, True)
-
-    pch, pcl = split(pc[...])
-    gp[...] = dot3s((pch, pcl), (pch, pcl), LAST)
-    grs[pl.ds(q, 1)] = gp[chunk(q), :][None]
-    start_all(gram_copy)
+    wait_chunk(gf, gf_sem, q, p != 0)
+    start_all(gram_all)
 
     col_finish(pr, pr_sem, True)
     prh, prl = split(pr[...])
@@ -341,25 +347,24 @@
     lax.fori_loop(0, 4, product, 0)
 
     out.go(wp.at[:, 1 - c], r1, r1_sem, (zh * 8 + x * 2 + 1 - c, q))
-    wait_slots(grs, grs_sem, q)
-    gf[chunk(q), :] = jnp.sum(grs[...], axis=0)
-    start_all(gram_all)
     arrived(r1, r1_sem)
     t[...] = wp[:, pl.ds(c, 1)][:, 0] + r1[...]
     for phase, z in ((0, 1 - zh), (1, zh)):
         for i in (1, 3, 2):
             xx = lax.rem(x + i, 4)
             out.go(t.at[z * 4 + xx], r2.at[phase, i - 1], r2_sem.at[phase, i - 1], (zh * 8 + xx * 2 + c, q))
-    for i in (1, 3, 2):
-        arrived(r2.at[0, i - 1], r2_sem.at[0, i - 1])
-    u[...] = t[(1 - zh) * 4 + x] + (r2[0, 0] + r2[0, 1] + r2[0, 2])
-    out.go(u, r3, r3_sem, ((1 - zh) * 8 + j, q))
     wait_chunks(gf, gf_sem, q)
     row = lax.broadcasted_iota(jnp.int32, (NB, NB), 0)
     col = lax.broadcasted_iota(jnp.int32, (NB, NB), 1)
     aug[:, 0:NB] = gf[...]
     aug[:, NB:] = (row == col).astype(F32)
     factor_block(aug, 0)
+    factor_block(aug, 1)
+    for i in (1, 3, 2):
+        arrived(r2.at[0, i - 1], r2_sem.at[0, i - 1])
+    u[...] = t[(1 - zh) * 4 + x] + (r2[0, 0] + r2[0, 1] + r2[0, 2])
+    out.go(u, r3, r3_sem, ((1 - zh) * 8 + j, q))
+    factor_block(aug, 2)
     for i in (1, 3, 2):
         arrived(r2.at[1, i - 1], r2_sem.at[1, i - 1])
     part = t[zh * 4 + x] + (r2[1, 0] + r2[1, 1] + r2[1, 2])
@@ -367,6 +372,10 @@
     mine = part + r3[...]
     wc[chunk(p), :] = mine
 
+    curv = cf.reshape(2, 4, 2, CH, NB)
+    c0[...] = dot3(mine, pc[...], LAST)
+    for i in (1, 3, 2):
+        out.go(c0, cy.at[i - 1], cy_sem.at[i - 1], (p, col_of(0, i)))
     out.go(wc.at[chunk(p)], wr.at[chunk(p)], wr_sem.at[p], (q, p), p != q)
     row_start(wc, wc_sem)
 
@@ -374,22 +383,20 @@
     def _():
         wr[chunk(q), :] = mine
 
-    crs[pl.ds(q, 1)] = dot3s(split(mine), (pch, pcl), LAST)[None]
-    start_all(curv_copy)
-    factor_block(aug, 1)
+    for i in (1, 3, 2):
+        arrived(cy.at[i - 1], cy_sem.at[i - 1])
+    c1[...] = c0[...] + (cy[0] + cy[1] + cy[2])
+    for i in (1, 3, 2):
+        out.go(c1, cz.at[i - 1], cz_sem.at[i - 1], (p, col_of(i, 0)))
+    factor_block(aug, 3)
     wait_chunk(wr, wr_sem, q, p != q)
     col_z(wr, wr_sem, False)
     col_y(wr, wr_sem, False, 0)
+    for i in (1, 3, 2):
+        arrived(cz.at[i - 1], cz_sem.at[i - 1])
+    cf[chunk(p), :] = c1[...] + (cz[0] + cz[1] + cz[2])
+    out.go(cf.at[chunk(p)], cf.at[chunk(p)], cf_sem.at[0], (row_of(1 - zh, 0, c), q))
     row_partner(wc, wc_sem)
-    factor_block(aug, 2)
-    for i in (1, 3, 2):
-        col_y(wr, wr_sem, False, i)
-    row_own(wc, wc_sem, zh)
-    wait_slots(crs, crs_sem, q)
-    cf[chunk(p), :] = jnp.sum(crs[...], axis=0)
-    start_all(curv_all)
-    factor_block(aug, 3)
-    row_own(wc, wc_sem, 1 - zh)
     rfac[...] = jnp.where(row <= col, aug[:, 0:NB], 0.0)
     inverse = aug[:, NB:]
     m = split(2.0 * dot6(inverse, inverse, FIRST))
@@ -397,11 +404,21 @@
     ah, al = split(ac[...])
     right[NB : 2 * NB, :] = ah
     right[3 * NB : 4 * NB, :] = al
+    for i in (1, 3, 2):
+        col_y(wr, wr_sem, False, i)
+    arrived(cf.at[chunk(row_of(1 - zh, 0, c))], cf_sem.at[0])
+    for i in (1, 3, 2):
+        out.go(curv.at[:, x, c], curv.at[:, x, c], cf_sem.at[i], (row_of(zh, i, c), q))
+    row_own(wc, wc_sem, zh)
     rh, rl = split(dot3s(m, split(pr[...]), PLAIN).T)
     left[:, 0:NB] = rh
     left[:, 2 * NB : 3 * NB] = rl
-
-    wait_chunks(cf, cf_sem, p)
+    for i in (1, 3, 2):
+        arrived(curv.at[:, lax.rem(x + 4 - i, 4), c], cf_sem.at[i])
+    out.go(curv.at[:, :, c], curv.at[:, :, c], cf_sem.at[4], (row_of(zh, 0, 1 - c), q))
+    row_own(wc, wc_sem, 1 - zh)
+    arrived(curv.at[:, :, 1 - c], cf_sem.at[4])
+
     turned = dot3s(split(cf[...]), (ah, al), PLAIN)
     row_finish(wc, wc_sem)
     vh, vl = split(wc[...] - turned)
@@ -412,8 +429,13 @@
     left[:, NB : 2 * NB] = vh
     left[:, 3 * NB : 4 * NB] = vl
     out.drain()
-    for make in (gram_copy, gram_all, curv_copy, curv_all):
-        drain_all(make)
+
+    @pl.when(p == 0)
+    def _():
+        drain_all(gram_copy)
+        drain_all(gram_down)
+
+    drain_all(gram_all)
 
 
 def exchange(matrix):
@@ -441,12 +463,15 @@
             pltpu.VMEM((CH, N), F32),
             small,
             pltpu.VMEM((16, CH, NB), F32),
-            pltpu.VMEM((16, CH, NB), F32),
+            pltpu.VMEM((CH, NB), F32),
+            pltpu.VMEM((CH, NB), F32),
+            pltpu.VMEM((3, CH, NB), F32),
+            pltpu.VMEM((3, CH, NB), F32),
             pltpu.VMEM((NB, 2 * NB), F32),
             big,
-            dma, dma((96,)), dma((16,)), dma((16,)), dma((16,)), dma((16,)),
+            dma, dma((112,)), dma((16,)), dma((16,)), dma((16,)),
             dma((16,)), dma((8,)), dma((16,)), dma((16,)), dma, dma((2, 3)), dma,
-            dma((16,)), dma((16,)), dma((16,)), dma((16,)),
+            dma((16,)), dma((16,)), dma((3,)), dma((3,)), dma((5,)),
         ],
         compiler_params=pltpu.CompilerParams(collective_id=0, has_side_effects=True, vmem_limit_bytes=48 << 20),
         name="exchange",

time: 102 us -> 99.9 us (0.979)
  the two profiles are of different devices: /device:TPU:127 before, /device:TPU:25 now
where the time goes in v4:
time: 99.9 us; the launch traced here: 99.8 us
  Pallas kernels  99.1 us (99%)
    pallas_call x1, Pallas kernels, exchange(): pl.pallas_call(exchange_kernel, out_shape=(jax.ShapeDtypeStruct((N, 4 * N...  92.9 us
    pallas_call x1, Pallas kernels, finish(): pl.pallas_call(finish_kernel, grid=(N // TILE,), out_shape=(jax.ShapeDtyp...  6.19 us

profile of v4, /device:TPU:25, one launch (start us, length us, event | category | flops | bytes accessed | tf_op | source)
XLA Modules:
  0.0 99.8 jit_solution(7605818128822092620)
XLA Ops:
  0.6 0.0 copy-start
  0.6 92.9 %exchange.1 = (bf16[1024,1024]{1,0:T(8,128)(2,1)S(1)}, bf16[1024,1024]{1,0:T(8,128)(2,1)S(1)}, f32[256,256]{1,0:T(8,128)S(1)}) custom-call(f32[1024,1024]{1,0:T(8,128)} %s.1), custom_call_target="tpu_custom_call" | custom-call | tf_op jit(solution)/shard_map/exchange/pallas_call | solution.py:446
  93.6 0.0 copy-done
  93.6 6.2 %finish.1 = (f32[1024,1024]{1,0:T(8,128)}, f32[256,256]{1,0:T(8,128)}) custom-call(bf16[1024,1024]{1,0:T(8,128)(2,1)S(1)} %get-tuple-element.5.left, bf16[1024,1024]{1,0:T(8,128)(2,1)S(1)} %get-tuple-element.6.right, f32[256,256]{1,0:T(8,128)S(1)} %get-tuple-element.7.factor, f32[1024,1024]{1,0:T(8,128)S(1)} %copy-done), custom_call_target="tpu_custom_call" | custom-call | tf_op jit(solution)/shard_map/finish/pallas_call | solution.py:496
Async XLA Ops:
  0.6 93.0 %copy-start = (f32[1024,1024]{1,0:T(8,128)S(1)}, f32[1024,1024]{1,0:T(8,128)}, u32[]{:S(2)}) copy-start(f32[1024,1024]{1,0:T(8,128)} %s.1) | copy-start | bytes 12582916

commit v5 on v4

--- a/solution.py
+++ b/solution.py
@@ -327,9 +327,9 @@
         gf[chunk(q), :] = jnp.sum(grs[...], axis=0)
         start_all(gram_down)
 
+    line(2, zl >= 0)
     pair_wait(pc, pc_sem, j, far)
     pair_spread(pc, pc_sem, far)
-    line(2, zl >= 0)
     line(3, zl >= 0)
     pair_forward(pc, pc_sem, True)
     pair_finish(pc, pc_sem, True)
@@ -359,12 +359,11 @@
     aug[:, 0:NB] = gf[...]
     aug[:, NB:] = (row == col).astype(F32)
     factor_block(aug, 0)
-    factor_block(aug, 1)
     for i in (1, 3, 2):
         arrived(r2.at[0, i - 1], r2_sem.at[0, i - 1])
     u[...] = t[(1 - zh) * 4 + x] + (r2[0, 0] + r2[0, 1] + r2[0, 2])
     out.go(u, r3, r3_sem, ((1 - zh) * 8 + j, q))
-    factor_block(aug, 2)
+    factor_block(aug, 1)
     for i in (1, 3, 2):
         arrived(r2.at[1, i - 1], r2_sem.at[1, i - 1])
     part = t[zh * 4 + x] + (r2[1, 0] + r2[1, 1] + r2[1, 2])
@@ -383,6 +382,7 @@
     def _():
         wr[chunk(q), :] = mine
 
+    factor_block(aug, 2)
     for i in (1, 3, 2):
         arrived(cy.at[i - 1], cy_sem.at[i - 1])
     c1[...] = c0[...] + (cy[0] + cy[1] + cy[2])
@@ -478,27 +478,35 @@
     )(matrix)
 
 
-def finish_kernel(left, right, factor, s, out, r):
-    rows = pl.ds(pl.multiple_of(pl.program_id(0) * TILE, TILE), TILE)
+TILE = 128
+
+
+def finish_kernel(left, right, factor, s, out, r, buf, sems, r_sem):
+    r_copy = pltpu.make_async_copy(factor, r, r_sem)
+    r_copy.start()
     half = 2 * NB
-    lh, ll = left[rows, 0:half], left[rows, half:]
-    rh, rl = right[0:half, :], right[half:, :]
-    out[...] = s[...] - (dot(lh, rh, PLAIN) + (dot(lh, rl, PLAIN) + dot(ll, rh, PLAIN)))
-    r[...] = factor[...]
-
-
-TILE = 128
+    copies = []
+    for i in range(N // TILE):
+        rows = slice(i * TILE, (i + 1) * TILE)
+        lh, ll = left[rows, 0:half], left[rows, half:]
+        rh, rl = right[0:half, :], right[half:, :]
+        buf[rows, :] = s[rows, :] - (dot(lh, rh, PLAIN) + (dot(lh, rl, PLAIN) + dot(ll, rh, PLAIN)))
+        copies.append(pltpu.make_async_copy(buf.at[rows], out.at[rows], sems.at[i]))
+        copies[-1].start()
+    for copy in copies:
+        copy.wait()
+    r_copy.wait()
 
 
 def finish(left, right, factor, matrix):
-    whole = lambda a: pl.BlockSpec(a.shape, lambda i: (0, 0))
-    tile = pl.BlockSpec((TILE, N), lambda i: (i, 0))
+    vm, anywhere = pl.BlockSpec(memory_space=pltpu.VMEM), pl.BlockSpec(memory_space=pl.ANY)
+    dma = pltpu.SemaphoreType.DMA
     return pl.pallas_call(
         finish_kernel,
-        grid=(N // TILE,),
         out_shape=(jax.ShapeDtypeStruct((N, N), F32), jax.ShapeDtypeStruct((NB, NB), F32)),
-        in_specs=[whole(left), whole(right), whole(factor), tile],
-        out_specs=(tile, whole(factor)),
+        in_specs=[vm] * 4,
+        out_specs=(anywhere, anywhere),
+        scratch_shapes=[pltpu.VMEM((N, N), F32), dma((N // TILE,)), dma],
         compiler_params=pltpu.CompilerParams(vmem_limit_bytes=32 << 20),
         name="finish",
     )(left, right, factor, matrix)

time: 99.9 us -> 92 us (0.921)
  the two profiles are of different devices: /device:TPU:25 before, /device:TPU:1 now
where the time goes in v5:
time: 92 us; the launch traced here: 91.9 us
  Pallas kernels  91.1 us (99%)
    pallas_call x1, Pallas kernels, exchange(): pl.pallas_call(exchange_kernel, out_shape=(jax.ShapeDtypeStruct((N, 4 * N...  86.8 us
    pallas_call x1, Pallas kernels, finish(): pl.pallas_call(finish_kernel, out_shape=(jax.ShapeDtypeStruct((N, N), F32...  4.31 us

profile of v5, /device:TPU:1, one launch (start us, length us, event | category | flops | bytes accessed | tf_op | source)
XLA Modules:
  0.0 91.9 jit_solution(36311596575460044)
XLA Ops:
  0.6 0.0 copy-start
  0.6 86.8 %exchange.1 = (bf16[1024,1024]{1,0:T(8,128)(2,1)S(1)}, bf16[1024,1024]{1,0:T(8,128)(2,1)S(1)}, f32[256,256]{1,0:T(8,128)S(1)}) custom-call(f32[1024,1024]{1,0:T(8,128)} %s.1), custom_call_target="tpu_custom_call" | custom-call | tf_op jit(solution)/shard_map/exchange/pallas_call | solution.py:446
  87.4 0.0 copy-done
  87.5 4.3 %finish.1 = (f32[1024,1024]{1,0:T(8,128)}, f32[256,256]{1,0:T(8,128)}) custom-call(bf16[1024,1024]{1,0:T(8,128)(2,1)S(1)} %get-tuple-element.5.left, bf16[1024,1024]{1,0:T(8,128)(2,1)S(1)} %get-tuple-element.6.right, f32[256,256]{1,0:T(8,128)S(1)} %get-tuple-element.7.factor, f32[1024,1024]{1,0:T(8,128)S(1)} %copy-done), custom_call_target="tpu_custom_call" | custom-call | tf_op jit(solution)/shard_map/finish/pallas_call | solution.py:504
Async XLA Ops:
  0.6 86.8 %copy-start = (f32[1024,1024]{1,0:T(8,128)S(1)}, f32[1024,1024]{1,0:T(8,128)}, u32[]{:S(2)}) copy-start(f32[1024,1024]{1,0:T(8,128)} %s.1) | copy-start | bytes 12582916

commit v6 on v5

--- a/solution.py
+++ b/solution.py
@@ -179,7 +179,7 @@
         k = col_of(i, 0)
         if i:
             wait_chunk(buf, sems, k, (q != 0) if root else None)
-        for n in (1, 3, 2):
+        for n in (2, 1, 3):
             d = col_of(0, n)
             send_chunk(buf, sems, k, (p, d), (d != 0) if root else None)
 
@@ -309,7 +309,7 @@
         k = i * 4 + y
         wait_chunk(pr, pr_sem, k, here & (q != 0))
         send_chunk(pr, pr_sem, k, (p, lax.rem(q + 4, 16)), here & (zl < 3))
-        for n in (1, 3, 2):
+        for n in (2, 1, 3):
             d = col_of(0, n)
             send_chunk(pr, pr_sem, k, (p, d), here & (d != 0))
 
@@ -388,10 +388,10 @@
     c1[...] = c0[...] + (cy[0] + cy[1] + cy[2])
     for i in (1, 3, 2):
         out.go(c1, cz.at[i - 1], cz_sem.at[i - 1], (p, col_of(i, 0)))
-    factor_block(aug, 3)
     wait_chunk(wr, wr_sem, q, p != q)
     col_z(wr, wr_sem, False)
     col_y(wr, wr_sem, False, 0)
+    factor_block(aug, 3)
     for i in (1, 3, 2):
         arrived(cz.at[i - 1], cz_sem.at[i - 1])
     cf[chunk(p), :] = c1[...] + (cz[0] + cz[1] + cz[2])

time: 92 us -> 92.1 us (level)
  no operation moved by 1% of the time
where the time goes in v6:
time: 92.1 us
  Pallas kernels  91.3 us (99%)
    pallas_call x1, Pallas kernels, exchange(): pl.pallas_call(exchange_kernel, out_shape=(jax.ShapeDtypeStruct((N, 4 * N...  86.9 us
    pallas_call x1, Pallas kernels, finish(): pl.pallas_call(finish_kernel, out_shape=(jax.ShapeDtypeStruct((N, N), F32...  4.31 us

profile of v6, /device:TPU:1, one launch (start us, length us, event | category | flops | bytes accessed | tf_op | source)
XLA Modules:
  0.0 92.1 jit_solution(4143057135408198701)
XLA Ops:
  0.6 0.0 copy-start
  0.6 86.9 %exchange.1 = (bf16[1024,1024]{1,0:T(8,128)(2,1)S(1)}, bf16[1024,1024]{1,0:T(8,128)(2,1)S(1)}, f32[256,256]{1,0:T(8,128)S(1)}) custom-call(f32[1024,1024]{1,0:T(8,128)} %s.1), custom_call_target="tpu_custom_call" | custom-call | tf_op jit(solution)/shard_map/exchange/pallas_call | solution.py:446
  87.6 0.0 copy-done
  87.6 4.3 %finish.1 = (f32[1024,1024]{1,0:T(8,128)}, f32[256,256]{1,0:T(8,128)}) custom-call(bf16[1024,1024]{1,0:T(8,128)(2,1)S(1)} %get-tuple-element.5.left, bf16[1024,1024]{1,0:T(8,128)(2,1)S(1)} %get-tuple-element.6.right, f32[256,256]{1,0:T(8,128)S(1)} %get-tuple-element.7.factor, f32[1024,1024]{1,0:T(8,128)S(1)} %copy-done), custom_call_target="tpu_custom_call" | custom-call | tf_op jit(solution)/shard_map/finish/pallas_call | solution.py:504
Async XLA Ops:
  0.6 87.0 %copy-start = (f32[1024,1024]{1,0:T(8,128)S(1)}, f32[1024,1024]{1,0:T(8,128)}, u32[]{:S(2)}) copy-start(f32[1024,1024]{1,0:T(8,128)} %s.1) | copy-start | bytes 12582916

commit v7 on v5

--- a/solution.py
+++ b/solution.py
@@ -344,10 +344,14 @@
         wp.reshape(NB, N)[:, cols] = dot3s((prh, prl), split(s[:, cols]), PLAIN)
         return z
 
-    lax.fori_loop(0, 4, product, 0)
-
-    out.go(wp.at[:, 1 - c], r1, r1_sem, (zh * 8 + x * 2 + 1 - c, q))
-    arrived(r1, r1_sem)
+    for part in (0, 1):
+        lax.fori_loop(2 * part, 2 * part + 2, product, 0)
+        cols = pl.ds(part * 512, 512)
+        out.go(
+            wp.at[:, 1 - c, :, cols], r1.at[:, :, cols], r1_sem.at[part], (zh * 8 + x * 2 + 1 - c, q)
+        )
+    for part in (0, 1):
+        arrived(r1.at[:, :, pl.ds(part * 512, 512)], r1_sem.at[part])
     t[...] = wp[:, pl.ds(c, 1)][:, 0] + r1[...]
     for phase, z in ((0, 1 - zh), (1, zh)):
         for i in (1, 3, 2):
@@ -470,7 +474,7 @@
             pltpu.VMEM((NB, 2 * NB), F32),
             big,
             dma, dma((112,)), dma((16,)), dma((16,)), dma((16,)),
-            dma((16,)), dma((8,)), dma((16,)), dma((16,)), dma, dma((2, 3)), dma,
+            dma((16,)), dma((8,)), dma((16,)), dma((16,)), dma((2,)), dma((2, 3)), dma,
             dma((16,)), dma((16,)), dma((3,)), dma((3,)), dma((5,)),
         ],
         compiler_params=pltpu.CompilerParams(collective_id=0, has_side_effects=True, vmem_limit_bytes=48 << 20),

time: 92 us -> 92 us (level)
  no operation moved by 1% of the time
where the time goes in v7:
time: 92 us; the launch traced here: 91.6 us
  Pallas kernels  90.8 us (99%)
    pallas_call x1, Pallas kernels, exchange(): pl.pallas_call(exchange_kernel, out_shape=(jax.ShapeDtypeStruct((N, 4 * N...  86.5 us
    pallas_call x1, Pallas kernels, finish(): pl.pallas_call(finish_kernel, out_shape=(jax.ShapeDtypeStruct((N, N), F32...  4.31 us

profile of v7, /device:TPU:1, one launch (start us, length us, event | category | flops | bytes accessed | tf_op | source)
XLA Modules:
  0.0 91.6 jit_solution(13651381632559661493)
XLA Ops:
  0.6 0.0 copy-start
  0.6 86.5 %exchange.1 = (bf16[1024,1024]{1,0:T(8,128)(2,1)S(1)}, bf16[1024,1024]{1,0:T(8,128)(2,1)S(1)}, f32[256,256]{1,0:T(8,128)S(1)}) custom-call(f32[1024,1024]{1,0:T(8,128)} %s.1), custom_call_target="tpu_custom_call" | custom-call | tf_op jit(solution)/shard_map/exchange/pallas_call | solution.py:450
  87.1 0.0 copy-done
  87.1 4.3 %finish.1 = (f32[1024,1024]{1,0:T(8,128)}, f32[256,256]{1,0:T(8,128)}) custom-call(bf16[1024,1024]{1,0:T(8,128)(2,1)S(1)} %get-tuple-element.5.left, bf16[1024,1024]{1,0:T(8,128)(2,1)S(1)} %get-tuple-element.6.right, f32[256,256]{1,0:T(8,128)S(1)} %get-tuple-element.7.factor, f32[1024,1024]{1,0:T(8,128)S(1)} %copy-done), custom_call_target="tpu_custom_call" | custom-call | tf_op jit(solution)/shard_map/finish/pallas_call | solution.py:508
Async XLA Ops:
  0.6 86.5 %copy-start = (f32[1024,1024]{1,0:T(8,128)S(1)}, f32[1024,1024]{1,0:T(8,128)}, u32[]{:S(2)}) copy-start(f32[1024,1024]{1,0:T(8,128)} %s.1) | copy-start | bytes 12582916
